TPU v7x, 32 devices: a whole 2x2x4 slice. The times are simulated.
32 devices in a mesh: func: 4 (over z), box: 8 (over y, x, core).
Axes of the slice: x: 2, y: 2, z: 4, core: 2. Of those that a mesh axis runs over, the one named last changes fastest.
Arguments:
- coeffs: bfloat16 [768, 32, 1024], P(('func', 'box')), may hold values from -8 to 8
- centers: int32 [768], replicated, may hold values from 0 to 383, as said below
- kinetic: bfloat16 [1024, 1024], replicated, may hold values from -0.1875 to 0.1875
- potential: float32 [384, 1024], P(('func', 'box')), may hold values from -1 to 1
Outputs:
- filtered: bfloat16 [768, 32, 1024], P(('func', 'box'))
- gram_band: float32 [768, 256], P(('func', 'box'))
Inputs may be any that keep to these rules, and one draw needn't show every extreme that they name: `centers`: centers never fall. The boxes form aligned groups of 32, and the groups aligned blocks of four; every box of a group is the center of the same number of functions, 1, 2 or 4, and each block of four groups holds the numbers 1, 1, 2 and 4 in an order whose running total of (number - 2) stays between -1 and 1. So between 32 and 128 functions touch each box, and some box is touched by exactly 128.
All inputs are finite; a program needn't handle non-finite values.
Results may differ from a plain program's by a relative error of at most 0.0057.
Values may be sent and summed in bfloat16 or wider, within the bound.
No kernel may reach another device: no remote copies, remote signals or barrier semaphores. Data moves between devices by JAX's collectives and lax.ppermute only.
A program may use at most 64 MiB of HBM per device.

v0:
```python
import jax
import jax.numpy as jnp
from jax import lax
from jax.sharding import PartitionSpec as P


def passed_along(value, axis, steps):
    count = lax.axis_size(axis)
    pairs = [(source, (source + steps) % count) for source in range(count)]
    return lax.ppermute(value, axis, pairs)


def to_band(matrix):
    leading = matrix.shape[:-2]
    matrix_order = matrix.shape[-1]
    spaces = [(0, 0)] * len(leading)
    padded = jnp.pad(matrix, spaces + [(0, 0), (matrix_order - 1, 1)])
    flattened = padded.reshape(leading + (2 * matrix_order * matrix_order,))
    flattened = jnp.pad(flattened, spaces + [(0, matrix_order)])
    return flattened.reshape(leading + (matrix_order, 2 * matrix_order + 1))[
        ..., : 2 * matrix_order
    ]


def from_band(band_rows):
    leading = band_rows.shape[:-2]
    matrix_order = band_rows.shape[-2]
    flattened = band_rows.reshape(leading + (2 * matrix_order * matrix_order,))
    flattened = flattened[..., : matrix_order * (2 * matrix_order - 1)]
    return flattened.reshape(leading + (matrix_order, 2 * matrix_order - 1))[
        ..., matrix_order - 1 :
    ]


def on_device(coeffs, centers, kinetic, potential):
    fun_dev, support, points = coeffs.shape
    devices = lax.axis_size(("func", "box"))
    my_index = lax.axis_index(("func", "box"))
    fun_all = fun_dev * devices
    box_dev = fun_dev // 2
    box_all = box_dev * devices
    capacity = 4 * support
    volume = 1.0 / (support * points)
    back_reach = (support // 2 + box_dev - 1) // box_dev
    span = back_reach + 2 + (3 * support // 2 - 2) // box_dev
    my_centers = lax.dynamic_slice_in_dim(centers, my_index * fun_dev, fun_dev)
    slot_range = jnp.arange(span, dtype=jnp.int32)
    local_box = jnp.arange(box_dev, dtype=jnp.int32)
    fun_range = jnp.arange(fun_dev, dtype=jnp.int32)
    step_range = jnp.arange(support, dtype=jnp.int32)
    target_dev = (my_index - back_reach + slot_range) % devices
    target_box = target_dev[:, None] * box_dev + local_box[None, :]
    step_out = (target_box[:, None, :] - my_centers[None, :, None]) % box_all
    select_out = (step_out[:, :, :, None] == step_range[None, None, None, :]).astype(jnp.bfloat16)
    outgoing = jnp.einsum(
        "jfks,fsp->jfkp", select_out, coeffs, preferred_element_type=jnp.float32
    ).astype(jnp.bfloat16)
    arrived = []
    for k in range(span):
        if k == back_reach:
            arrived.append(outgoing[k])
        else:
            arrived.append(passed_along(outgoing[k], ("func", "box"), k - back_reach))
    received = jnp.stack(arrived)
    received_rows = received.reshape(span * fun_dev, box_dev, points)
    box_ids = my_index * box_dev + local_box
    window_start = (box_ids - support + 1) % box_all
    first_row = jnp.searchsorted(centers, window_start, side="left")
    end_row = jnp.searchsorted(centers, box_ids + 1, side="left")
    filled = (end_row - first_row) % fun_all
    slot_ids = jnp.arange(capacity, dtype=jnp.int32)
    row_ids = (first_row[:, None] + slot_ids[None, :]) % fun_all
    live_slot = slot_ids[None, :] < filled[:, None]
    sender = row_ids // fun_dev
    slot_of = jnp.minimum((my_index + back_reach - sender) % devices, span - 1)
    source_row = slot_of * fun_dev + row_ids % fun_dev
    row_range = jnp.arange(span * fun_dev, dtype=jnp.int32)
    select_in = jnp.logical_and(
        live_slot[..., None], source_row[..., None] == row_range[None, None, :]
    ).astype(jnp.bfloat16)
    box_pieces = jnp.einsum(
        "kmr,rkp->kmp", select_in, received_rows, preferred_element_type=jnp.float32
    ).astype(jnp.bfloat16)
    gram_box = volume * jnp.einsum(
        "kmp,knp->kmn", box_pieces, box_pieces, preferred_element_type=jnp.float32
    )
    band_rows = to_band(gram_box)
    masked_rows = jnp.where(live_slot[..., None], band_rows, 0.0)
    source_dev = (my_index + back_reach - slot_range) % devices
    fun_ids = source_dev[:, None] * fun_dev + fun_range[None, :]
    position = (fun_ids[:, :, None] - first_row[None, None, :]) % fun_all
    live_back = position < filled[None, None, :]
    select_back = jnp.logical_and(
        live_back[..., None], position[..., None] == slot_ids[None, None, None, :]
    )
    term_back = jnp.einsum(
        "jfkm,kmc->jfc",
        select_back.astype(jnp.float32),
        masked_rows,
        precision=lax.Precision.HIGHEST,
    )
    gram_band = term_back[back_reach]
    for k in range(span):
        if k != back_reach:
            gram_band = gram_band + passed_along(term_back[k], ("func", "box"), back_reach - k)
    diag_mask = (jnp.arange(2 * capacity) == capacity - 1).astype(jnp.float32)
    mine_rows = (1.5 * diag_mask - 0.5 * gram_band).astype(jnp.bfloat16)
    row_list = []
    for k in range(span):
        if k == back_reach:
            row_list.append(mine_rows)
        else:
            row_list.append(passed_along(mine_rows, ("func", "box"), k - back_reach))
    rows_here = jnp.stack(row_list)
    rows_flat = rows_here.reshape(span * fun_dev, 2 * capacity)
    select_rows = (source_row[..., None] == row_range[None, None, :]).astype(jnp.bfloat16)
    slot_rows = jnp.einsum(
        "kmr,rc->kmc", select_rows, rows_flat, preferred_element_type=jnp.float32
    ).astype(jnp.bfloat16)
    mixing = from_band(slot_rows)
    corrected = jnp.einsum(
        "kml,klp->kmp", mixing, box_pieces, preferred_element_type=jnp.float32
    ).astype(jnp.bfloat16)
    applied = jnp.einsum("kmp,pq->kmq", corrected, kinetic, preferred_element_type=jnp.float32)
    applied = (applied + potential[:, None, :] * corrected.astype(jnp.float32)).astype(jnp.bfloat16)
    backward = jnp.einsum(
        "jfkm,kmp->jfkp",
        select_back.astype(jnp.bfloat16),
        applied,
        preferred_element_type=jnp.float32,
    ).astype(jnp.bfloat16)
    coming = []
    for k in range(span):
        if k == back_reach:
            coming.append(backward[k])
        else:
            coming.append(passed_along(backward[k], ("func", "box"), back_reach - k))
    returned = jnp.stack(coming)
    piece_box = (my_centers[:, None] + step_range[None, :]) % box_all
    slot_back = (piece_box // box_dev - my_index + back_reach) % devices
    select_home = jnp.logical_and(
        slot_back[:, :, None, None] == slot_range[None, None, :, None],
        (piece_box % box_dev)[:, :, None, None] == local_box[None, None, None, :],
    ).astype(jnp.bfloat16)
    filtered = jnp.einsum(
        "fsjk,jfkp->fsp", select_home, returned, preferred_element_type=jnp.float32
    ).astype(jnp.bfloat16)
    return (filtered, gram_band)


def solution(mesh):
    placed = (P(("func", "box"), None, None), P(), P(), P(("func", "box"), None))
    return jax.shard_map(
        on_device,
        mesh=mesh,
        in_specs=placed,
        out_specs=(P(("func", "box"), None, None), P(("func", "box"), None)),
        check_vma=False,
    )
```

profile of v0, /device:TPU:20, one launch (start us, length us, event | category | flops | bytes accessed | tf_op | source)
XLA Modules:
  0.0 242.8 jit_solution(4591362407807593816)
XLA Ops:
  1.8 3.3 %convert_bitcast_fusion = bf16[7,24,12,1024]{3,2,0,1:T(8,128)(2,1)S(1)} fusion(bf16[24,32,1024]{2,1,0:T(8,128)(2,1)} %param.8, s32[7,24,12]{2,0,1:T(8,128)S(1)} %copy.58), kind=kOutput, calls=%fused_computation.22 | convolution fusion | flops 134249472 | bytes 5709696 | tf_op jit(solution)/shard_map/jfks,fsp->jfkp/dot_general | solution.py:55
  10.6 7.1 %while.37 = (s32[]{:T(128)}, u32[12]{0:T(128)S(1)}, u32[12]{0:T(128)S(1)}, s32[768]{0:T(1024)S(1)}, s32[]{:T(128)}, /*index=5*/s32[]{:T(128)}, s32[]{:T(128)}, s32[]{}) while((s32[]{:T(128)}, u32[12]{0:T(128)S(1)}, u32[12]{0:T(128)S(1)}, s32[768]{0:T(1024)S(1)}, s32[]{:T(128)}, /*index=5*/s32[]{:T(128)}, s32[]{:T(128)}, s32[]{}) %tuple.87), condition=%wide.region_1.2_spmd.clone, body=%wide.region_0.1_spmd.clone.sunk | while | flops 1280 | bytes 4784 | solution.py:68
  17.8 7.1 %while.38 = (s32[]{:T(128)}, u32[12]{0:T(128)S(1)}, u32[12]{0:T(128)S(1)}, s32[768]{0:T(1024)S(1)}, s32[]{:T(128)}, /*index=5*/s32[]{:T(128)}, s32[]{:T(128)}, s32[]{}) while((s32[]{:T(128)}, u32[12]{0:T(128)S(1)}, u32[12]{0:T(128)S(1)}, s32[768]{0:T(1024)S(1)}, s32[]{:T(128)}, /*index=5*/s32[]{:T(128)}, s32[]{:T(128)}, s32[]{}) %tuple.88), condition=%wide.region_3.4_spmd.clone, body=%wide.region_2.3_spmd.clone.sunk | while | flops 1208 | bytes 4784 | solution.py:69
  25.4 3.1 %collective-permute-done.1 = bf16[24,12,1024]{2,0,1:T(8,128)(2,1)} collective-permute-done((bf16[24,12,1024]{2,0,1:T(8,128)(2,1)}, bf16[24,12,1024]{2,0,1:T(8,128)(2,1)}, u32[]{:S(2)}, u32[]{:S(2)}) %collective-permute-start.1) | collective-permute-done | bytes 589856 | tf_op jit(solution)/shard_map/ppermute | solution.py:10
  34.2 3.3 %collective-permute-start.3 = (bf16[24,12,1024]{2,0,1:T(8,128)(2,1)S(1)}, bf16[24,12,1024]{2,0,1:T(8,128)(2,1)S(1)}, u32[]{:S(2)}, u32[]{:S(2)}) collective-permute-start(bf16[24,12,1024]{2,0,1:T(8,128)(2,1)S(1)} %copy.65), channel_id=1, source_target_pairs={{0,2},{1,3},{2,4},{3,5},{4,6},{5,7},{6,8},{7,9},{8,10},{9,11},{10,... | collective-permute-start | bytes 1769480 | tf_op jit(solution)/shard_map/ppermute | solution.py:10
  39.3 8.5 %collective-permute-done.2 = bf16[24,12,1024]{2,0,1:T(8,128)(2,1)S(1)} collective-permute-done((bf16[24,12,1024]{2,0,1:T(8,128)(2,1)S(1)}, bf16[24,12,1024]{2,0,1:T(8,128)(2,1)S(1)}, u32[]{:S(2)}, u32[]{:S(2)}) %collective-permute-start.2) | collective-permute-done | bytes 589856 | tf_op jit(solution)/shard_map/ppermute | solution.py:10
  48.1 3.3 %collective-permute-done.3 = bf16[24,12,1024]{2,0,1:T(8,128)(2,1)S(1)} collective-permute-done((bf16[24,12,1024]{2,0,1:T(8,128)(2,1)S(1)}, bf16[24,12,1024]{2,0,1:T(8,128)(2,1)S(1)}, u32[]{:S(2)}, u32[]{:S(2)}) %collective-permute-start.3) | collective-permute-done | bytes 589856 | tf_op jit(solution)/shard_map/ppermute | solution.py:10
  51.8 22.9 %collective-permute-done.4 = bf16[24,12,1024]{2,0,1:T(8,128)(2,1)S(1)} collective-permute-done((bf16[24,12,1024]{2,0,1:T(8,128)(2,1)S(1)}, bf16[24,12,1024]{2,0,1:T(8,128)(2,1)S(1)}, u32[]{:S(2)}, u32[]{:S(2)}) %collective-permute-start.4) | collective-permute-done | bytes 589856 | tf_op jit(solution)/shard_map/ppermute | solution.py:10
  83.4 4.0 %reshape.277 = f32[12,128,257]{2,1,0:T(8,128)} reshape(f32[12,32896]{1,0:T(8,128)} %pad.9) | data formatting | bytes 3158016 | tf_op jit(solution)/shard_map/reshape | solution.py:20
  90.2 8.0 %collective-permute-start.10 = (f32[24,256]{1,0:T(8,128)S(1)}, f32[24,256]{1,0:T(8,128)S(1)}, u32[]{:S(2)}, u32[]{:S(2)}) collective-permute-start(f32[24,256]{1,0:T(8,128)S(1)} %get-tuple-element.207), channel_id=1, source_target_pairs={{0,29},{1,30},{2,31},{3,0},{4,1},{5,2},{6,3},{7,4},{8,5},{9,6},{10... | collective-permute-start | bytes 73736 | tf_op jit(solution)/shard_map/ppermute | solution.py:10
  98.1 16.5 %collective-permute-start.6 = (f32[24,256]{1,0:T(8,128)S(1)}, f32[24,256]{1,0:T(8,128)S(1)}, u32[]{:S(2)}, u32[]{:S(2)}) collective-permute-start(f32[24,256]{1,0:T(8,128)S(1)} %get-tuple-element.205), channel_id=1, source_target_pairs={{0,2},{1,3},{2,4},{3,5},{4,6},{5,7},{6,8},{7,9},{8,10},{9,11},{10,... | collective-permute-start | bytes 73736 | tf_op jit(solution)/shard_map/ppermute | solution.py:10
  126.6 3.7 %collective-permute-start.16 = (bf16[24,256]{1,0:T(8,128)(2,1)S(1)}, bf16[24,256]{1,0:T(8,128)(2,1)S(1)}, u32[]{:S(2)}, u32[]{:S(2)}) collective-permute-start(bf16[24,256]{1,0:T(8,128)(2,1)S(1)} %get-tuple-element.186), channel_id=1, source_target_pairs={{0,3},{1,4},{2,5},{3,6},{4,7},{5,8},{6,9},{7,10},{8,11},{9,12},{10... | collective-permute-start | bytes 36872 | tf_op jit(solution)/shard_map/ppermute | solution.py:10
  130.2 5.7 %collective-permute-start.17 = (bf16[24,256]{1,0:T(8,128)(2,1)S(1)}, bf16[24,256]{1,0:T(8,128)(2,1)S(1)}, u32[]{:S(2)}, u32[]{:S(2)}) collective-permute-start(bf16[24,256]{1,0:T(8,128)(2,1)S(1)} %get-tuple-element.186), channel_id=1, source_target_pairs={{0,4},{1,5},{2,6},{3,7},{4,8},{5,9},{6,10},{7,11},{8,12},{9,13},{1... | collective-permute-start | bytes 36872 | tf_op jit(solution)/shard_map/ppermute | solution.py:10
  138.7 3.4 %reshape.280 = bf16[12,128,255]{2,1,0:T(8,128)(2,1)} reshape(bf16[12,32640]{1,0:T(8,128)(2,1)S(1)} %slice.115) | data formatting | bytes 1566720 | tf_op jit(solution)/shard_map/reshape | solution.py:30
  142.2 4.8 %fusion.41 = bf16[12,128,1024]{2,1,0:T(8,128)(2,1)} fusion(bf16[12,128,1024]{2,1,0:T(8,128)(2,1)} %copy-done.2, bf16[12,128,255]{2,1,0:T(8,128)(2,1)} %reshape.280), kind=kOutput, calls=%fused_computation.79 | convolution fusion | flops 402653184 | bytes 6684672 | tf_op jit(solution)/shard_map/kml,klp->kmp/dot_general | solution.py:121
  147.0 9.6 %fusion.11 = f32[12,1024,168]{1,2,0} fusion(pred[12,128,168]{1,2,0:T(8,128)(4,1)S(1)} %bitcast.155, f32[12,1024]{1,0:T(8,128)S(1)} %copy-done.4, bf16[12,128,1024]{2,1,0:T(8,128)(2,1)} %fusion.41, bf16[1024,1024]{1,0:T(8,128)(2,1)S(1)} %copy-done), kind=kOutput, calls=%fused_computation.24 | convolution fusion | flops 3755999232 | bytes 13807616
  156.6 4.0 %convert_bitcast_fusion.1 = bf16[7,24,12,1024]{3,1,0,2:T(8,128)(2,1)S(1)} fusion(f32[12,1024,7,24]{1,3,2,0:T(8,128)} %bitcast.152), kind=kLoop, calls=%fused_computation.23 | loop fusion | flops 2064384 | bytes 12386304 | tf_op jit(solution)/shard_map/convert_element_type | solution.py:131
  161.0 5.7 %collective-permute-start.18 = (bf16[24,12,1024]{2,0,1:T(8,128)(2,1)S(1)}, bf16[24,12,1024]{2,0,1:T(8,128)(2,1)S(1)}, u32[]{:S(2)}, u32[]{:S(2)}) collective-permute-start(bf16[24,12,1024]{2,0,1:T(8,128)(2,1)S(1)} %get-tuple-element.203), channel_id=1, source_target_pairs={{0,2},{1,3},{2,4},{3,5},{4,6},{5,7},{6,8},{7,9},{8,10},{9,11},{10,... | collective-permute-start | bytes 1769480 | tf_op jit(solution)/shard_map/ppermute | solution.py:10
  169.6 10.9 %collective-permute-done.18 = bf16[24,12,1024]{2,0,1:T(8,128)(2,1)S(1)} collective-permute-done((bf16[24,12,1024]{2,0,1:T(8,128)(2,1)S(1)}, bf16[24,12,1024]{2,0,1:T(8,128)(2,1)S(1)}, u32[]{:S(2)}, u32[]{:S(2)}) %collective-permute-start.18) | collective-permute-done | bytes 589856 | tf_op jit(solution)/shard_map/ppermute | solution.py:10
  180.5 5.9 %collective-permute-done.19 = bf16[24,12,1024]{2,0,1:T(8,128)(2,1)S(1)} collective-permute-done((bf16[24,12,1024]{2,0,1:T(8,128)(2,1)S(1)}, bf16[24,12,1024]{2,0,1:T(8,128)(2,1)S(1)}, u32[]{:S(2)}, u32[]{:S(2)}) %collective-permute-start.19) | collective-permute-done | bytes 589856 | tf_op jit(solution)/shard_map/ppermute | solution.py:10
  186.5 6.7 %collective-permute-done.20 = bf16[24,12,1024]{2,0,1:T(8,128)(2,1)S(1)} collective-permute-done((bf16[24,12,1024]{2,0,1:T(8,128)(2,1)S(1)}, bf16[24,12,1024]{2,0,1:T(8,128)(2,1)S(1)}, u32[]{:S(2)}, u32[]{:S(2)}) %collective-permute-start.20) | collective-permute-done | bytes 589856 | tf_op jit(solution)/shard_map/ppermute | solution.py:10
  193.2 13.2 %collective-permute-done.21 = bf16[24,12,1024]{2,0,1:T(8,128)(2,1)S(1)} collective-permute-done((bf16[24,12,1024]{2,0,1:T(8,128)(2,1)S(1)}, bf16[24,12,1024]{2,0,1:T(8,128)(2,1)S(1)}, u32[]{:S(2)}, u32[]{:S(2)}) %collective-permute-start.21) | collective-permute-done | bytes 589856 | tf_op jit(solution)/shard_map/ppermute | solution.py:10
  206.5 30.2 %collective-permute-done.23 = bf16[24,12,1024]{2,0,1:T(8,128)(2,1)S(1)} collective-permute-done((bf16[24,12,1024]{2,0,1:T(8,128)(2,1)S(1)}, bf16[24,12,1024]{2,0,1:T(8,128)(2,1)S(1)}, u32[]{:S(2)}, u32[]{:S(2)}) %collective-permute-start.23) | collective-permute-done | bytes 589856 | tf_op jit(solution)/shard_map/ppermute | solution.py:10
  236.8 6.0 %bitcast_convert_fusion = bf16[24,32,1024]{2,1,0:T(8,128)(2,1)} fusion(bf16[7,24,12,1024]{3,1,2,0:T(8,128)(2,1)S(1)} %bitcast_dynamic-update-slice_fusion.6, pred[24,32,12]{1,2,0:T(8,128)(4,1)S(1)} %iota_compare_fusion.5, pred[24,32,7]{1,2,0:T(8,128)(4,1)S(1)} %iota_compare_fusion.6), kind=kOutput, calls=%fused_computation.25 | convolution fusion | flops 132971520 | bytes 5716224 | tf_op jit(solution)/shard_map/fsjk,jfkp->fsp/dot_general | solution.py:145
  (188 shorter events, 58.3 us)
Async XLA Ops:
  8.0 17.1 %collective-permute-start = (bf16[24,12,1024]{2,0,1:T(8,128)(2,1)S(1)}, bf16[24,12,1024]{2,0,1:T(8,128)(2,1)S(1)}, u32[]{:S(2)}, u32[]{:S(2)}) collective-permute-start(bf16[24,12,1024]{2,0,1:T(8,128)(2,1)S(1)} %copy.59), channel_id=1, source_target_pairs={{0,30},{1,31},{2,0},{3,1},{4,2},{5,3},{6,4},{7,5},{8,6},{9,7},{10,... | collective-permute-start | bytes 1769480 | tf_op jit(solution)/shard_map/ppermute | solution.py:10
  10.6 17.9 %collective-permute-start.1 = (bf16[24,12,1024]{2,0,1:T(8,128)(2,1)}, bf16[24,12,1024]{2,0,1:T(8,128)(2,1)}, u32[]{:S(2)}, u32[]{:S(2)}) collective-permute-start(bf16[24,12,1024]{2,0,1:T(8,128)(2,1)} %copy.61), channel_id=1, source_target_pairs={{0,31},{1,0},{2,1},{3,2},{4,3},{5,4},{6,5},{7,6},{8,7},{9,8},{10,9... | collective-permute-start | bytes 1769480 | tf_op jit(solution)/shard_map/ppermute | solution.py:10
  32.8 15.0 %collective-permute-start.2 = (bf16[24,12,1024]{2,0,1:T(8,128)(2,1)S(1)}, bf16[24,12,1024]{2,0,1:T(8,128)(2,1)S(1)}, u32[]{:S(2)}, u32[]{:S(2)}) collective-permute-start(bf16[24,12,1024]{2,0,1:T(8,128)(2,1)S(1)} %copy.63), channel_id=1, source_target_pairs={{0,1},{1,2},{2,3},{3,4},{4,5},{5,6},{6,7},{7,8},{8,9},{9,10},{10,1... | collective-permute-start | bytes 1769480 | tf_op jit(solution)/shard_map/ppermute | solution.py:10
  34.2 17.3 %collective-permute-start.3 = (bf16[24,12,1024]{2,0,1:T(8,128)(2,1)S(1)}, bf16[24,12,1024]{2,0,1:T(8,128)(2,1)S(1)}, u32[]{:S(2)}, u32[]{:S(2)}) collective-permute-start(bf16[24,12,1024]{2,0,1:T(8,128)(2,1)S(1)} %copy.65), channel_id=1, source_target_pairs={{0,2},{1,3},{2,4},{3,5},{4,6},{5,7},{6,8},{7,9},{8,10},{9,11},{10,... | collective-permute-start | bytes 1769480 | tf_op jit(solution)/shard_map/ppermute | solution.py:10
  37.9 36.8 %collective-permute-start.4 = (bf16[24,12,1024]{2,0,1:T(8,128)(2,1)S(1)}, bf16[24,12,1024]{2,0,1:T(8,128)(2,1)S(1)}, u32[]{:S(2)}, u32[]{:S(2)}) collective-permute-start(bf16[24,12,1024]{2,0,1:T(8,128)(2,1)S(1)} %copy.67), channel_id=1, source_target_pairs={{0,3},{1,4},{2,5},{3,6},{4,7},{5,8},{6,9},{7,10},{8,11},{9,12},{10... | collective-permute-start | bytes 1769480 | tf_op jit(solution)/shard_map/ppermute | solution.py:10
  38.4 36.7 %collective-permute-start.5 = (bf16[24,12,1024]{2,0,1:T(8,128)(2,1)S(1)}, bf16[24,12,1024]{2,0,1:T(8,128)(2,1)S(1)}, u32[]{:S(2)}, u32[]{:S(2)}) collective-permute-start(bf16[24,12,1024]{2,0,1:T(8,128)(2,1)S(1)} %copy.69), channel_id=1, source_target_pairs={{0,4},{1,5},{2,6},{3,7},{4,8},{5,9},{6,10},{7,11},{8,12},{9,13},{1... | collective-permute-start | bytes 1769480 | tf_op jit(solution)/shard_map/ppermute | solution.py:10
  90.2 27.1 %collective-permute-start.10 = (f32[24,256]{1,0:T(8,128)S(1)}, f32[24,256]{1,0:T(8,128)S(1)}, u32[]{:S(2)}, u32[]{:S(2)}) collective-permute-start(f32[24,256]{1,0:T(8,128)S(1)} %get-tuple-element.207), channel_id=1, source_target_pairs={{0,29},{1,30},{2,31},{3,0},{4,1},{5,2},{6,3},{7,4},{8,5},{9,6},{10... | collective-permute-start | bytes 73736 | tf_op jit(solution)/shard_map/ppermute | solution.py:10
  98.1 19.6 %collective-permute-start.11 = (f32[24,256]{1,0:T(8,128)S(1)}, f32[24,256]{1,0:T(8,128)S(1)}, u32[]{:S(2)}, u32[]{:S(2)}) collective-permute-start(f32[24,256]{1,0:T(8,128)S(1)} %get-tuple-element.206), channel_id=1, source_target_pairs={{0,28},{1,29},{2,30},{3,31},{4,0},{5,1},{6,2},{7,3},{8,4},{9,5},{1... | collective-permute-start | bytes 73736 | tf_op jit(solution)/shard_map/ppermute | solution.py:10
  98.1 19.6 %collective-permute-start.6 = (f32[24,256]{1,0:T(8,128)S(1)}, f32[24,256]{1,0:T(8,128)S(1)}, u32[]{:S(2)}, u32[]{:S(2)}) collective-permute-start(f32[24,256]{1,0:T(8,128)S(1)} %get-tuple-element.205), channel_id=1, source_target_pairs={{0,2},{1,3},{2,4},{3,5},{4,6},{5,7},{6,8},{7,9},{8,10},{9,11},{10,... | collective-permute-start | bytes 73736 | tf_op jit(solution)/shard_map/ppermute | solution.py:10
  114.6 4.2 %collective-permute-start.7 = (f32[24,256]{1,0:T(8,128)S(1)}, f32[24,256]{1,0:T(8,128)S(1)}, u32[]{:S(2)}, u32[]{:S(2)}) collective-permute-start(f32[24,256]{1,0:T(8,128)S(1)} %get-tuple-element.210), channel_id=1, source_target_pairs={{0,1},{1,2},{2,3},{3,4},{4,5},{5,6},{6,7},{7,8},{8,9},{9,10},{10,1... | collective-permute-start | bytes 73736 | tf_op jit(solution)/shard_map/ppermute | solution.py:10
  114.6 4.2 %collective-permute-start.8 = (f32[24,256]{1,0:T(8,128)S(1)}, f32[24,256]{1,0:T(8,128)S(1)}, u32[]{:S(2)}, u32[]{:S(2)}) collective-permute-start(f32[24,256]{1,0:T(8,128)S(1)} %get-tuple-element.209), channel_id=1, source_target_pairs={{0,31},{1,0},{2,1},{3,2},{4,3},{5,4},{6,5},{7,6},{8,7},{9,8},{10,9... | collective-permute-start | bytes 73736 | tf_op jit(solution)/shard_map/ppermute | solution.py:10
  117.3 3.8 %collective-permute-start.9 = (f32[24,256]{1,0:T(8,128)S(1)}, f32[24,256]{1,0:T(8,128)S(1)}, u32[]{:S(2)}, u32[]{:S(2)}) collective-permute-start(f32[24,256]{1,0:T(8,128)S(1)} %get-tuple-element.208), channel_id=1, source_target_pairs={{0,30},{1,31},{2,0},{3,1},{4,2},{5,3},{6,4},{7,5},{8,6},{9,7},{10,... | collective-permute-start | bytes 73736 | tf_op jit(solution)/shard_map/ppermute | solution.py:10
  121.7 8.5 %collective-permute-start.12 = (bf16[24,256]{1,0:T(8,128)(2,1)S(1)}, bf16[24,256]{1,0:T(8,128)(2,1)S(1)}, u32[]{:S(2)}, u32[]{:S(2)}) collective-permute-start(bf16[24,256]{1,0:T(8,128)(2,1)S(1)} %get-tuple-element.186), channel_id=1, source_target_pairs={{0,30},{1,31},{2,0},{3,1},{4,2},{5,3},{6,4},{7,5},{8,6},{9,7},{10,... | collective-permute-start | bytes 36872 | tf_op jit(solution)/shard_map/ppermute | solution.py:10
  124.5 11.5 %collective-permute-start.13 = (bf16[24,256]{1,0:T(8,128)(2,1)S(1)}, bf16[24,256]{1,0:T(8,128)(2,1)S(1)}, u32[]{:S(2)}, u32[]{:S(2)}) collective-permute-start(bf16[24,256]{1,0:T(8,128)(2,1)S(1)} %get-tuple-element.186), channel_id=1, source_target_pairs={{0,31},{1,0},{2,1},{3,2},{4,3},{5,4},{6,5},{7,6},{8,7},{9,8},{10,9... | collective-permute-start | bytes 36872 | tf_op jit(solution)/shard_map/ppermute | solution.py:10
  124.5 11.4 %collective-permute-start.14 = (bf16[24,256]{1,0:T(8,128)(2,1)S(1)}, bf16[24,256]{1,0:T(8,128)(2,1)S(1)}, u32[]{:S(2)}, u32[]{:S(2)}) collective-permute-start(bf16[24,256]{1,0:T(8,128)(2,1)S(1)} %get-tuple-element.186), channel_id=1, source_target_pairs={{0,1},{1,2},{2,3},{3,4},{4,5},{5,6},{6,7},{7,8},{8,9},{9,10},{10,1... | collective-permute-start | bytes 36872 | tf_op jit(solution)/shard_map/ppermute | solution.py:10
  125.0 10.9 %collective-permute-start.15 = (bf16[24,256]{1,0:T(8,128)(2,1)S(1)}, bf16[24,256]{1,0:T(8,128)(2,1)S(1)}, u32[]{:S(2)}, u32[]{:S(2)}) collective-permute-start(bf16[24,256]{1,0:T(8,128)(2,1)S(1)} %get-tuple-element.186), channel_id=1, source_target_pairs={{0,2},{1,3},{2,4},{3,5},{4,6},{5,7},{6,8},{7,9},{8,10},{9,11},{10,... | collective-permute-start | bytes 36872 | tf_op jit(solution)/shard_map/ppermute | solution.py:10
  126.6 9.4 %collective-permute-start.16 = (bf16[24,256]{1,0:T(8,128)(2,1)S(1)}, bf16[24,256]{1,0:T(8,128)(2,1)S(1)}, u32[]{:S(2)}, u32[]{:S(2)}) collective-permute-start(bf16[24,256]{1,0:T(8,128)(2,1)S(1)} %get-tuple-element.186), channel_id=1, source_target_pairs={{0,3},{1,4},{2,5},{3,6},{4,7},{5,8},{6,9},{7,10},{8,11},{9,12},{10... | collective-permute-start | bytes 36872 | tf_op jit(solution)/shard_map/ppermute | solution.py:10
  130.2 7.1 %collective-permute-start.17 = (bf16[24,256]{1,0:T(8,128)(2,1)S(1)}, bf16[24,256]{1,0:T(8,128)(2,1)S(1)}, u32[]{:S(2)}, u32[]{:S(2)}) collective-permute-start(bf16[24,256]{1,0:T(8,128)(2,1)S(1)} %get-tuple-element.186), channel_id=1, source_target_pairs={{0,4},{1,5},{2,6},{3,7},{4,8},{5,9},{6,10},{7,11},{8,12},{9,13},{1... | collective-permute-start | bytes 36872 | tf_op jit(solution)/shard_map/ppermute | solution.py:10
  161.0 19.5 %collective-permute-start.18 = (bf16[24,12,1024]{2,0,1:T(8,128)(2,1)S(1)}, bf16[24,12,1024]{2,0,1:T(8,128)(2,1)S(1)}, u32[]{:S(2)}, u32[]{:S(2)}) collective-permute-start(bf16[24,12,1024]{2,0,1:T(8,128)(2,1)S(1)} %get-tuple-element.203), channel_id=1, source_target_pairs={{0,2},{1,3},{2,4},{3,5},{4,6},{5,7},{6,8},{7,9},{8,10},{9,11},{10,... | collective-permute-start | bytes 1769480 | tf_op jit(solution)/shard_map/ppermute | solution.py:10
  166.8 19.6 %collective-permute-start.19 = (bf16[24,12,1024]{2,0,1:T(8,128)(2,1)S(1)}, bf16[24,12,1024]{2,0,1:T(8,128)(2,1)S(1)}, u32[]{:S(2)}, u32[]{:S(2)}) collective-permute-start(bf16[24,12,1024]{2,0,1:T(8,128)(2,1)S(1)} %get-tuple-element.202), channel_id=1, source_target_pairs={{0,1},{1,2},{2,3},{3,4},{4,5},{5,6},{6,7},{7,8},{8,9},{9,10},{10,1... | collective-permute-start | bytes 1769480 | tf_op jit(solution)/shard_map/ppermute | solution.py:10
  166.9 26.2 %collective-permute-start.20 = (bf16[24,12,1024]{2,0,1:T(8,128)(2,1)S(1)}, bf16[24,12,1024]{2,0,1:T(8,128)(2,1)S(1)}, u32[]{:S(2)}, u32[]{:S(2)}) collective-permute-start(bf16[24,12,1024]{2,0,1:T(8,128)(2,1)S(1)} %get-tuple-element.201), channel_id=1, source_target_pairs={{0,31},{1,0},{2,1},{3,2},{4,3},{5,4},{6,5},{7,6},{8,7},{9,8},{10,9... | collective-permute-start | bytes 1769480 | tf_op jit(solution)/shard_map/ppermute | solution.py:10
  169.6 36.8 %collective-permute-start.21 = (bf16[24,12,1024]{2,0,1:T(8,128)(2,1)S(1)}, bf16[24,12,1024]{2,0,1:T(8,128)(2,1)S(1)}, u32[]{:S(2)}, u32[]{:S(2)}) collective-permute-start(bf16[24,12,1024]{2,0,1:T(8,128)(2,1)S(1)} %get-tuple-element.200), channel_id=1, source_target_pairs={{0,30},{1,31},{2,0},{3,1},{4,2},{5,3},{6,4},{7,5},{8,6},{9,7},{10,... | collective-permute-start | bytes 1769480 | tf_op jit(solution)/shard_map/ppermute | solution.py:10
  169.6 36.9 %collective-permute-start.22 = (bf16[24,12,1024]{2,0,1:T(8,128)(2,1)S(1)}, bf16[24,12,1024]{2,0,1:T(8,128)(2,1)S(1)}, u32[]{:S(2)}, u32[]{:S(2)}) collective-permute-start(bf16[24,12,1024]{2,0,1:T(8,128)(2,1)S(1)} %get-tuple-element.204), channel_id=1, source_target_pairs={{0,29},{1,30},{2,31},{3,0},{4,1},{5,2},{6,3},{7,4},{8,5},{9,6},{10... | collective-permute-start | bytes 1769480 | tf_op jit(solution)/shard_map/ppermute | solution.py:10
  180.4 56.3 %collective-permute-start.23 = (bf16[24,12,1024]{2,0,1:T(8,128)(2,1)S(1)}, bf16[24,12,1024]{2,0,1:T(8,128)(2,1)S(1)}, u32[]{:S(2)}, u32[]{:S(2)}) collective-permute-start(bf16[24,12,1024]{2,0,1:T(8,128)(2,1)S(1)} %get-tuple-element.199), channel_id=1, source_target_pairs={{0,28},{1,29},{2,30},{3,31},{4,0},{5,1},{6,2},{7,3},{8,4},{9,5},{1... | collective-permute-start | bytes 1769480 | tf_op jit(solution)/shard_map/ppermute | solution.py:10
  (5 other events, 161.8 us)
where the time goes:
time: 243 us
  waiting for transfers between devices  109 us (45%)
  starting transfers between devices  56.1 us (23%)
  local copies, waits for them, and re-layouts  39.6 us (16%)
  matrix products  29.1 us (12%)
  other arithmetic  6.77 us (3%)
    ppermute x24, waiting for transfers between devices, passed_along(): return lax.ppermute(value, axis, pairs)  109 us
    ppermute x24, starting transfers between devices, passed_along(): return lax.ppermute(value, axis, pairs)  56.1 us
    gather x20, local copies, waits for them, and re-layouts, on_device(): first_row = jnp.searchsorted(centers, window_start, side='left')  12.8 us
    unnamed x1, matrix products  9.6 us
    unnamed x31, local copies, waits for them, and re-layouts  7.68 us
    dot_general x1, matrix products, on_device(): jnp.einsum('fsjk,jfkp->fsp', select_home, returned, preferred_element_typ...  5.95 us
    squeeze x8, local copies, waits for them, and re-layouts, on_device(): arrived.append(passed_along(outgoing[k], ('func', 'box'), k - back_reach))  5.46 us
  transfers between devices with their start and end apart: 24, of which 13 were waited for; matrix products, arithmetic and copies ran while one was open for 8% of the time, Pallas kernels for 0%

commit v1 on v0

v1 whole, which is shorter than its diff:
```python
import jax
import jax.numpy as jnp
from jax import lax
from jax.sharding import PartitionSpec as P

AXES = ("func", "box")


def passed_along(value, steps):
    count = lax.axis_size(AXES)
    pairs = [(source, (source + steps) % count) for source in range(count)]
    return lax.ppermute(value, AXES, pairs)


def on_device(coeffs, centers, kinetic, potential):
    fun_dev, support, points = coeffs.shape
    devices = lax.axis_size(AXES)
    me = lax.axis_index(AXES)
    box_dev = fun_dev // 2
    box_all = box_dev * devices
    volume = 1.0 / (support * points)
    shift = 1
    reach = 3
    offsets = list(range(-reach, reach + 1))
    order = sorted(offsets, key=lambda k: (abs(k), k))
    span = len(offsets)
    window = span * fun_dev
    reading = 4 * support

    my_potential = passed_along(potential, -shift)
    my_centers = lax.dynamic_slice_in_dim(centers, me * fun_dev, fun_dev)
    local_box = jnp.arange(box_dev, dtype=jnp.int32)
    steps = jnp.arange(support, dtype=jnp.int32)
    target = (me + shift + jnp.array(offsets, jnp.int32)) % devices
    target_box = target[:, None] * box_dev + local_box[None, :]
    step_out = (target_box[:, None, :] - my_centers[None, :, None]) % box_all
    select = (step_out[..., None] == steps).astype(jnp.bfloat16)
    outgoing = jnp.einsum(
        "jfks,fsp->jfkp", select, coeffs, preferred_element_type=jnp.float32
    ).astype(jnp.bfloat16)
    arrived = [None] * span
    for k in order:
        piece = outgoing[k + reach]
        arrived[reach - k] = piece if k == 0 else passed_along(piece, k)
    pieces = jnp.concatenate([a.reshape(fun_dev, box_dev * points) for a in arrived], axis=0)
    partial = volume * lax.dot_general(
        pieces, pieces, (((1,), (1,)), ((), ())), preferred_element_type=jnp.float32
    )
    total = partial
    wide = (2 * span - 1) * fun_dev
    rows = jnp.pad(partial[reach * fun_dev : (reach + 1) * fun_dev], ((0, 0), (reach * fun_dev, reach * fun_dev)))
    for k in order:
        if k == 0:
            continue
        other = passed_along(partial, k)
        at = -k * fun_dev
        total = total + lax.pad(other, 0.0, ((at, -at, 0), (at, -at, 0)))
        row_at = (reach + k) * fun_dev
        rows = rows + jnp.pad(other[row_at : row_at + fun_dev], ((0, 0), ((reach - k) * fun_dev, (reach + k) * fun_dev)))
    first = (2 * reach) * fun_dev - (reading - 1)
    gram_band = jnp.stack([rows[r, first + r : first + r + 2 * reading] for r in range(fun_dev)])
    last = (jnp.arange(2 * reading) < 2 * reading - 1)
    gram_band = jnp.where(last, gram_band, 0.0)
    diag = jnp.eye(window, dtype=jnp.float32)
    correction = (1.5 * diag - 0.5 * total).astype(jnp.bfloat16)
    corrected = lax.dot_general(
        correction, pieces, (((1,), (0,)), ((), ())), preferred_element_type=jnp.float32
    ).astype(jnp.bfloat16).reshape(window, box_dev, points)
    applied = jnp.einsum("fbp,pq->fbq", corrected, kinetic, preferred_element_type=jnp.float32)
    applied = (applied + my_potential[None] * corrected.astype(jnp.float32)).astype(jnp.bfloat16)
    coming = [None] * span
    for k in order:
        piece = applied[(reach - k) * fun_dev : (reach - k + 1) * fun_dev]
        coming[k + reach] = piece if k == 0 else passed_along(piece, -k)
    returned = jnp.stack(coming)
    filtered = jnp.einsum(
        "jfks,jfkp->fsp", select, returned, preferred_element_type=jnp.float32
    ).astype(jnp.bfloat16)
    return (filtered, gram_band)


def solution(mesh):
    placed = (P(AXES, None, None), P(), P(), P(AXES, None))
    return jax.shard_map(
        on_device,
        mesh=mesh,
        in_specs=placed,
        out_specs=(P(AXES, None, None), P(AXES, None)),
        check_vma=False,
    )
```

time: 243 us -> 171 us (0.70)
  the two profiles are of different devices: /device:TPU:20 before, /device:TPU:1 now
where the time goes in v1:
time: 171 us; the launch traced here: 167 us
  waiting for transfers between devices  76.8 us (45%)
  starting transfers between devices  54.7 us (32%)
  matrix products  18.6 us (11%)
  local copies, waits for them, and re-layouts  13.4 us (8%)
  other arithmetic  2.73 us (2%)
    ppermute x19, waiting for transfers between devices, passed_along(): return lax.ppermute(value, AXES, pairs)  76.8 us
    ppermute x19, starting transfers between devices, passed_along(): return lax.ppermute(value, AXES, pairs)  54.7 us
    dot_general x1, matrix products, on_device(): jnp.einsum('jfks,jfkp->fsp', select, returned, preferred_element_type=jnp...  7.86 us
    unnamed x19, local copies, waits for them, and re-layouts  6.15 us
    dot_general x1, matrix products, on_device(): jnp.einsum('fbp,pq->fbq', corrected, kinetic, preferred_element_type=jnp....  4.7 us
  transfers between devices with their start and end apart: 19, of which 6 were waited for; matrix products, arithmetic and copies ran while one was open for 7% of the time, Pallas kernels for 0%

profile of v1, /device:TPU:1, one launch (start us, length us, event | category | flops | bytes accessed | tf_op | source)
XLA Modules:
  0.0 167.3 jit_solution(2011018993306138509)
XLA Ops:
  2.4 3.3 %convert_bitcast_fusion = bf16[7,24,12,1024]{3,2,0,1:T(8,128)(2,1)S(1)} fusion(bf16[24,32,1024]{2,1,0:T(8,128)(2,1)} %param.5, s32[7,24,12]{2,0,1:T(8,128)S(1)} %add_select_fusion), kind=kOutput, calls=%fused_computation.4 | convolution fusion | flops 134249472 | bytes 5709696 | tf_op jit(solution)/shard_map/jfks,fsp->jfkp/dot_general | solution.py:38
  7.2 2.7 %collective-permute-start = (bf16[24,12,1024]{2,0,1:T(8,128)(2,1)S(1)}, bf16[24,12,1024]{2,0,1:T(8,128)(2,1)S(1)}, u32[]{:S(2)}, u32[]{:S(2)}) collective-permute-start(bf16[24,12,1024]{2,0,1:T(8,128)(2,1)S(1)} %copy.13), channel_id=1, source_target_pairs={{0,3},{1,4},{2,5},{3,6},{4,7},{5,8},{6,9},{7,10},{8,11},{9,12},{10... | collective-permute-start | bytes 1769480 | tf_op jit(solution)/shard_map/ppermute | solution.py:12
  10.2 1.3 collective-permute-start.1
  11.8 1.2 collective-permute-start.2
  13.8 3.9 %collective-permute-start.4 = (bf16[24,12,1024]{2,0,1:T(8,128)(2,1)S(1)}, bf16[24,12,1024]{2,0,1:T(8,128)(2,1)S(1)}, u32[]{:S(2)}, u32[]{:S(2)}) collective-permute-start(bf16[24,12,1024]{2,0,1:T(8,128)(2,1)S(1)} %copy.21), channel_id=1, source_target_pairs={{0,30},{1,31},{2,0},{3,1},{4,2},{5,3},{6,4},{7,5},{8,6},{9,7},{10,... | collective-permute-start | bytes 1769480 | tf_op jit(solution)/shard_map/ppermute | solution.py:12
  18.0 24.0 %collective-permute-done = bf16[24,12,1024]{2,0,1:T(8,128)(2,1)S(1)} collective-permute-done((bf16[24,12,1024]{2,0,1:T(8,128)(2,1)S(1)}, bf16[24,12,1024]{2,0,1:T(8,128)(2,1)S(1)}, u32[]{:S(2)}, u32[]{:S(2)}) %collective-permute-start) | collective-permute-done | bytes 589856 | tf_op jit(solution)/shard_map/ppermute | solution.py:12
  42.4 1.3 collective-permute-done.1
  43.7 17.2 %collective-permute-done.2 = bf16[24,12,1024]{2,0,1:T(8,128)(2,1)S(1)} collective-permute-done((bf16[24,12,1024]{2,0,1:T(8,128)(2,1)S(1)}, bf16[24,12,1024]{2,0,1:T(8,128)(2,1)S(1)}, u32[]{:S(2)}, u32[]{:S(2)}) %collective-permute-start.2) | collective-permute-done | bytes 589856 | tf_op jit(solution)/shard_map/ppermute | solution.py:12
  61.5 1.3 convolution_multiply_fusion
  62.8 6.5 %collective-permute-start.11 = (f32[168,168]{1,0:T(8,128)S(1)}, f32[168,168]{1,0:T(8,128)S(1)}, u32[]{:S(2)}, u32[]{:S(2)}) collective-permute-start(f32[168,168]{1,0:T(8,128)S(1)} %convolution_multiply_fusion), channel_id=1, source_target_pairs={{0,3},{1,4},{2,5},{3,6},{4,7},{5,8},{6,9},{7,10},{8,11},{9,12},{10... | collective-permute-start | bytes 338696 | tf_op jit(solution)/shard_map/ppermute | solution.py:12
  69.3 8.9 %collective-permute-start.10 = (f32[168,168]{1,0:T(8,128)S(1)}, f32[168,168]{1,0:T(8,128)S(1)}, u32[]{:S(2)}, u32[]{:S(2)}) collective-permute-start(f32[168,168]{1,0:T(8,128)S(1)} %convolution_multiply_fusion), channel_id=1, source_target_pairs={{0,29},{1,30},{2,31},{3,0},{4,1},{5,2},{6,3},{7,4},{8,5},{9,6},{10... | collective-permute-start | bytes 338696 | tf_op jit(solution)/shard_map/ppermute | solution.py:12
  78.3 5.1 %collective-permute-start.8 = (f32[168,168]{1,0:T(8,128)S(1)}, f32[168,168]{1,0:T(8,128)S(1)}, u32[]{:S(2)}, u32[]{:S(2)}) collective-permute-start(f32[168,168]{1,0:T(8,128)S(1)} %convolution_multiply_fusion), channel_id=1, source_target_pairs={{0,30},{1,31},{2,0},{3,1},{4,2},{5,3},{6,4},{7,5},{8,6},{9,7},{10,... | collective-permute-start | bytes 338696 | tf_op jit(solution)/shard_map/ppermute | solution.py:12
  83.3 2.3 %collective-permute-start.6 = (f32[168,168]{1,0:T(8,128)S(1)}, f32[168,168]{1,0:T(8,128)S(1)}, u32[]{:S(2)}, u32[]{:S(2)}) collective-permute-start(f32[168,168]{1,0:T(8,128)S(1)} %convolution_multiply_fusion), channel_id=1, source_target_pairs={{0,31},{1,0},{2,1},{3,2},{4,3},{5,4},{6,5},{7,6},{8,7},{9,8},{10,9... | collective-permute-start | bytes 338696 | tf_op jit(solution)/shard_map/ppermute | solution.py:12
  85.6 1.4 collective-permute-start.12
  87.0 5.0 %collective-permute-done.7 = f32[168,168]{1,0:T(8,128)S(1)} collective-permute-done((f32[168,168]{1,0:T(8,128)S(1)}, f32[168,168]{1,0:T(8,128)S(1)}, u32[]{:S(2)}, u32[]{:S(2)}) %collective-permute-start.7) | collective-permute-done | bytes 112928 | tf_op jit(solution)/shard_map/ppermute | solution.py:12
  92.8 1.5 convolution_convert_fusion
  94.4 4.7 %add_convert_fusion = bf16[168,12,1024]{2,0,1:T(8,128)(2,1)S(1)} fusion(f32[12,1024]{1,0:T(8,128)S(1)} %collective-permute-done.12, bf16[21,12,8,1024]{3,2,1,0:T(8,128)(2,1)S(1)} %bitcast.67, bf16[1024,1024]{1,0:T(8,128)(2,1)S(1)} %copy-done), kind=kOutput, calls=%fused_computation.1 | convolution fusion | flops 4236115968 | bytes 10403840 | tf_op jit(solution)/shard_map/fbp,pq->fbq/dot_general | solution.py:69
  99.1 1.8 %fusion.35 = (bf16[24,12,1024]{2,0,1:T(8,128)(2,1)S(1)}, bf16[24,12,1024]{2,0,1:T(8,128)(2,1)S(1)}, bf16[24,12,1024]{2,0,1:T(8,128)(2,1)}, bf16[24,12,1024]{2,0,...) fusion(bf16[168,12,1024]{2,0,1:T(8,128)(2,1)S(1)} %add_convert_fusion), kind=kLoop, calls=%fused_computation.100 | loop fusion | bytes 7077888 | tf_op jit(solution)/shard_map/slice | solution.py:73
  101.0 5.4 %collective-permute-start.18 = (bf16[24,12,1024]{2,0,1:T(8,128)(2,1)S(1)}, bf16[24,12,1024]{2,0,1:T(8,128)(2,1)}, u32[]{:S(2)}, u32[]{:S(2)}) collective-permute-start(bf16[24,12,1024]{2,0,1:T(8,128)(2,1)S(1)} %get-tuple-element.9), channel_id=1, source_target_pairs={{0,29},{1,30},{2,31},{3,0},{4,1},{5,2},{6,3},{7,4},{8,5},{9,6},{10... | collective-permute-start | bytes 1769480 | tf_op jit(solution)/shard_map/ppermute | solution.py:12
  108.0 2.6 %collective-permute-start.14 = (bf16[24,12,1024]{2,0,1:T(8,128)(2,1)}, bf16[24,12,1024]{2,0,1:T(8,128)(2,1)}, u32[]{:S(2)}, u32[]{:S(2)}) collective-permute-start(bf16[24,12,1024]{2,0,1:T(8,128)(2,1)} %get-tuple-element.13), channel_id=1, source_target_pairs={{0,2},{1,3},{2,4},{3,5},{4,6},{5,7},{6,8},{7,9},{8,10},{9,11},{10,... | collective-permute-start | bytes 1769480 | tf_op jit(solution)/shard_map/ppermute | solution.py:12
  111.6 9.1 %collective-permute-done.13 = bf16[24,12,1024]{2,0,1:T(8,128)(2,1)} collective-permute-done((bf16[24,12,1024]{2,0,1:T(8,128)(2,1)}, bf16[24,12,1024]{2,0,1:T(8,128)(2,1)}, u32[]{:S(2)}, u32[]{:S(2)}) %collective-permute-start.13) | collective-permute-done | bytes 589856 | tf_op jit(solution)/shard_map/ppermute | solution.py:12
  120.7 11.8 %collective-permute-start.16 = (bf16[24,12,1024]{2,0,1:T(8,128)(2,1)}, bf16[24,12,1024]{2,0,1:T(8,128)(2,1)S(1)}, u32[]{:S(2)}, u32[]{:S(2)}) collective-permute-start(bf16[24,12,1024]{2,0,1:T(8,128)(2,1)} %get-tuple-element.11), channel_id=1, source_target_pairs={{0,31},{1,0},{2,1},{3,2},{4,3},{5,4},{6,5},{7,6},{8,7},{9,8},{10,9... | collective-permute-start | bytes 1769480 | tf_op jit(solution)/shard_map/ppermute | solution.py:12
  133.5 20.2 %collective-permute-done.14 = bf16[24,12,1024]{2,0,1:T(8,128)(2,1)} collective-permute-done((bf16[24,12,1024]{2,0,1:T(8,128)(2,1)}, bf16[24,12,1024]{2,0,1:T(8,128)(2,1)}, u32[]{:S(2)}, u32[]{:S(2)}) %collective-permute-start.14) | collective-permute-done | bytes 589856 | tf_op jit(solution)/shard_map/ppermute | solution.py:12
  159.4 7.9 %bitcast_convert_fusion = bf16[24,32,1024]{2,1,0:T(8,128)(2,1)} fusion(bf16[7,24,12,1024]{3,1,2,0:T(8,128)(2,1)S(1)} %bitcast_dynamic-update-slice_fusion, s32[7,24,12]{2,0,1:T(8,128)S(1)} %add_select_fusion), kind=kOutput, calls=%fused_computation.8 | convolution fusion | flops 132971520 | bytes 5709696 | tf_op jit(solution)/shard_map/jfks,jfkp->fsp/dot_general | solution.py:76
  (80 shorter events, 16.0 us)
Async XLA Ops:
  0.6 93.7 %copy-start = (bf16[1024,1024]{1,0:T(8,128)(2,1)S(1)}, bf16[1024,1024]{1,0:T(8,128)(2,1)}, u32[]{:S(2)}) copy-start(bf16[1024,1024]{1,0:T(8,128)(2,1)} %param.7) | copy-start | bytes 6291460
  7.2 34.8 %collective-permute-start = (bf16[24,12,1024]{2,0,1:T(8,128)(2,1)S(1)}, bf16[24,12,1024]{2,0,1:T(8,128)(2,1)S(1)}, u32[]{:S(2)}, u32[]{:S(2)}) collective-permute-start(bf16[24,12,1024]{2,0,1:T(8,128)(2,1)S(1)} %copy.13), channel_id=1, source_target_pairs={{0,3},{1,4},{2,5},{3,6},{4,7},{5,8},{6,9},{7,10},{8,11},{9,12},{10... | collective-permute-start | bytes 1769480 | tf_op jit(solution)/shard_map/ppermute | solution.py:12
  10.2 33.4 %collective-permute-start.1 = (bf16[24,12,1024]{2,0,1:T(8,128)(2,1)S(1)}, bf16[24,12,1024]{2,0,1:T(8,128)(2,1)S(1)}, u32[]{:S(2)}, u32[]{:S(2)}) collective-permute-start(bf16[24,12,1024]{2,0,1:T(8,128)(2,1)S(1)} %copy.15), channel_id=1, source_target_pairs={{0,2},{1,3},{2,4},{3,5},{4,6},{5,7},{6,8},{7,9},{8,10},{9,11},{10,... | collective-permute-start | bytes 1769480 | tf_op jit(solution)/shard_map/ppermute | solution.py:12
  11.8 49.1 %collective-permute-start.2 = (bf16[24,12,1024]{2,0,1:T(8,128)(2,1)S(1)}, bf16[24,12,1024]{2,0,1:T(8,128)(2,1)S(1)}, u32[]{:S(2)}, u32[]{:S(2)}) collective-permute-start(bf16[24,12,1024]{2,0,1:T(8,128)(2,1)S(1)} %copy.17), channel_id=1, source_target_pairs={{0,1},{1,2},{2,3},{3,4},{4,5},{5,6},{6,7},{7,8},{8,9},{9,10},{10,1... | collective-permute-start | bytes 1769480 | tf_op jit(solution)/shard_map/ppermute | solution.py:12
  13.4 47.6 %collective-permute-start.3 = (bf16[24,12,1024]{2,0,1:T(8,128)(2,1)S(1)}, bf16[24,12,1024]{2,0,1:T(8,128)(2,1)S(1)}, u32[]{:S(2)}, u32[]{:S(2)}) collective-permute-start(bf16[24,12,1024]{2,0,1:T(8,128)(2,1)S(1)} %copy.19), channel_id=1, source_target_pairs={{0,31},{1,0},{2,1},{3,2},{4,3},{5,4},{6,5},{7,6},{8,7},{9,8},{10,9... | collective-permute-start | bytes 1769480 | tf_op jit(solution)/shard_map/ppermute | solution.py:12
  13.8 47.3 %collective-permute-start.4 = (bf16[24,12,1024]{2,0,1:T(8,128)(2,1)S(1)}, bf16[24,12,1024]{2,0,1:T(8,128)(2,1)S(1)}, u32[]{:S(2)}, u32[]{:S(2)}) collective-permute-start(bf16[24,12,1024]{2,0,1:T(8,128)(2,1)S(1)} %copy.21), channel_id=1, source_target_pairs={{0,30},{1,31},{2,0},{3,1},{4,2},{5,3},{6,4},{7,5},{8,6},{9,7},{10,... | collective-permute-start | bytes 1769480 | tf_op jit(solution)/shard_map/ppermute | solution.py:12
  42.0 19.1 %collective-permute-start.5 = (bf16[24,12,1024]{2,0,1:T(8,128)(2,1)S(1)}, bf16[24,12,1024]{2,0,1:T(8,128)(2,1)S(1)}, u32[]{:S(2)}, u32[]{:S(2)}) collective-permute-start(bf16[24,12,1024]{2,0,1:T(8,128)(2,1)S(1)} %copy.23), channel_id=1, source_target_pairs={{0,29},{1,30},{2,31},{3,0},{4,1},{5,2},{6,3},{7,4},{8,5},{9,6},{10... | collective-permute-start | bytes 1769480 | tf_op jit(solution)/shard_map/ppermute | solution.py:12
  61.5 24.1 %copy-start.2 = (f32[12,1024]{1,0:T(8,128)S(1)}, f32[12,1024]{1,0:T(8,128)}, u32[]{:S(2)}) copy-start(f32[12,1024]{1,0:T(8,128)} %param.8) | copy-start | bytes 147460
  62.8 20.5 %collective-permute-start.11 = (f32[168,168]{1,0:T(8,128)S(1)}, f32[168,168]{1,0:T(8,128)S(1)}, u32[]{:S(2)}, u32[]{:S(2)}) collective-permute-start(f32[168,168]{1,0:T(8,128)S(1)} %convolution_multiply_fusion), channel_id=1, source_target_pairs={{0,3},{1,4},{2,5},{3,6},{4,7},{5,8},{6,9},{7,10},{8,11},{9,12},{10... | collective-permute-start | bytes 338696 | tf_op jit(solution)/shard_map/ppermute | solution.py:12
  69.3 16.3 %collective-permute-start.10 = (f32[168,168]{1,0:T(8,128)S(1)}, f32[168,168]{1,0:T(8,128)S(1)}, u32[]{:S(2)}, u32[]{:S(2)}) collective-permute-start(f32[168,168]{1,0:T(8,128)S(1)} %convolution_multiply_fusion), channel_id=1, source_target_pairs={{0,29},{1,30},{2,31},{3,0},{4,1},{5,2},{6,3},{7,4},{8,5},{9,6},{10... | collective-permute-start | bytes 338696 | tf_op jit(solution)/shard_map/ppermute | solution.py:12
  78.2 8.8 %collective-permute-start.9 = (f32[168,168]{1,0:T(8,128)S(1)}, f32[168,168]{1,0:T(8,128)S(1)}, u32[]{:S(2)}, u32[]{:S(2)}) collective-permute-start(f32[168,168]{1,0:T(8,128)S(1)} %convolution_multiply_fusion), channel_id=1, source_target_pairs={{0,2},{1,3},{2,4},{3,5},{4,6},{5,7},{6,8},{7,9},{8,10},{9,11},{10,... | collective-permute-start | bytes 338696 | tf_op jit(solution)/shard_map/ppermute | solution.py:12
  78.3 8.8 %collective-permute-start.8 = (f32[168,168]{1,0:T(8,128)S(1)}, f32[168,168]{1,0:T(8,128)S(1)}, u32[]{:S(2)}, u32[]{:S(2)}) collective-permute-start(f32[168,168]{1,0:T(8,128)S(1)} %convolution_multiply_fusion), channel_id=1, source_target_pairs={{0,30},{1,31},{2,0},{3,1},{4,2},{5,3},{6,4},{7,5},{8,6},{9,7},{10,... | collective-permute-start | bytes 338696 | tf_op jit(solution)/shard_map/ppermute | solution.py:12
  83.3 8.7 %collective-permute-start.7 = (f32[168,168]{1,0:T(8,128)S(1)}, f32[168,168]{1,0:T(8,128)S(1)}, u32[]{:S(2)}, u32[]{:S(2)}) collective-permute-start(f32[168,168]{1,0:T(8,128)S(1)} %convolution_multiply_fusion), channel_id=1, source_target_pairs={{0,1},{1,2},{2,3},{3,4},{4,5},{5,6},{6,7},{7,8},{8,9},{9,10},{10,1... | collective-permute-start | bytes 338696 | tf_op jit(solution)/shard_map/ppermute | solution.py:12
  83.3 8.7 %collective-permute-start.6 = (f32[168,168]{1,0:T(8,128)S(1)}, f32[168,168]{1,0:T(8,128)S(1)}, u32[]{:S(2)}, u32[]{:S(2)}) collective-permute-start(f32[168,168]{1,0:T(8,128)S(1)} %convolution_multiply_fusion), channel_id=1, source_target_pairs={{0,31},{1,0},{2,1},{3,2},{4,3},{5,4},{6,5},{7,6},{8,7},{9,8},{10,9... | collective-permute-start | bytes 338696 | tf_op jit(solution)/shard_map/ppermute | solution.py:12
  85.6 8.7 %collective-permute-start.12 = (f32[12,1024]{1,0:T(8,128)S(1)}, f32[12,1024]{1,0:T(8,128)S(1)}, u32[]{:S(2)}, u32[]{:S(2)}) collective-permute-start(f32[12,1024]{1,0:T(8,128)S(1)} %copy-done.2), channel_id=1, source_target_pairs={{0,31},{1,0},{2,1},{3,2},{4,3},{5,4},{6,5},{7,6},{8,7},{9,8},{10,9... | collective-permute-start | bytes 147464 | tf_op jit(solution)/shard_map/ppermute | solution.py:12
  99.1 11.9 %copy-start.1 = (bf16[168,12,1024]{2,0,1:T(8,128)(2,1)}, bf16[168,12,1024]{2,0,1:T(8,128)(2,1)S(1)}, u32[]{:S(2)}) copy-start(bf16[168,12,1024]{2,0,1:T(8,128)(2,1)S(1)} %add_convert_fusion) | copy-start | bytes 12386308
  100.9 19.8 %collective-permute-start.13 = (bf16[24,12,1024]{2,0,1:T(8,128)(2,1)}, bf16[24,12,1024]{2,0,1:T(8,128)(2,1)}, u32[]{:S(2)}, u32[]{:S(2)}) collective-permute-start(bf16[24,12,1024]{2,0,1:T(8,128)(2,1)} %get-tuple-element.14), channel_id=1, source_target_pairs={{0,3},{1,4},{2,5},{3,6},{4,7},{5,8},{6,9},{7,10},{8,11},{9,12},{10... | collective-permute-start | bytes 1769480 | tf_op jit(solution)/shard_map/ppermute | solution.py:12
  101.0 57.3 %collective-permute-start.18 = (bf16[24,12,1024]{2,0,1:T(8,128)(2,1)S(1)}, bf16[24,12,1024]{2,0,1:T(8,128)(2,1)}, u32[]{:S(2)}, u32[]{:S(2)}) collective-permute-start(bf16[24,12,1024]{2,0,1:T(8,128)(2,1)S(1)} %get-tuple-element.9), channel_id=1, source_target_pairs={{0,29},{1,30},{2,31},{3,0},{4,1},{5,2},{6,3},{7,4},{8,5},{9,6},{10... | collective-permute-start | bytes 1769480 | tf_op jit(solution)/shard_map/ppermute | solution.py:12
  106.4 50.8 %collective-permute-start.17 = (bf16[24,12,1024]{2,0,1:T(8,128)(2,1)S(1)}, bf16[24,12,1024]{2,0,1:T(8,128)(2,1)}, u32[]{:S(2)}, u32[]{:S(2)}) collective-permute-start(bf16[24,12,1024]{2,0,1:T(8,128)(2,1)S(1)} %get-tuple-element.10), channel_id=1, source_target_pairs={{0,30},{1,31},{2,0},{3,1},{4,2},{5,3},{6,4},{7,5},{8,6},{9,7},{10,... | collective-permute-start | bytes 1769480 | tf_op jit(solution)/shard_map/ppermute | solution.py:12
  107.5 47.4 %collective-permute-start.15 = (bf16[24,12,1024]{2,0,1:T(8,128)(2,1)}, bf16[24,12,1024]{2,0,1:T(8,128)(2,1)}, u32[]{:S(2)}, u32[]{:S(2)}) collective-permute-start(bf16[24,12,1024]{2,0,1:T(8,128)(2,1)} %get-tuple-element.12), channel_id=1, source_target_pairs={{0,1},{1,2},{2,3},{3,4},{4,5},{5,6},{6,7},{7,8},{8,9},{9,10},{10,1... | collective-permute-start | bytes 1769480 | tf_op jit(solution)/shard_map/ppermute | solution.py:12
  108.0 45.8 %collective-permute-start.14 = (bf16[24,12,1024]{2,0,1:T(8,128)(2,1)}, bf16[24,12,1024]{2,0,1:T(8,128)(2,1)}, u32[]{:S(2)}, u32[]{:S(2)}) collective-permute-start(bf16[24,12,1024]{2,0,1:T(8,128)(2,1)} %get-tuple-element.13), channel_id=1, source_target_pairs={{0,2},{1,3},{2,4},{3,5},{4,6},{5,7},{6,8},{7,9},{8,10},{9,11},{10,... | collective-permute-start | bytes 1769480 | tf_op jit(solution)/shard_map/ppermute | solution.py:12
  120.7 36.4 %collective-permute-start.16 = (bf16[24,12,1024]{2,0,1:T(8,128)(2,1)}, bf16[24,12,1024]{2,0,1:T(8,128)(2,1)S(1)}, u32[]{:S(2)}, u32[]{:S(2)}) collective-permute-start(bf16[24,12,1024]{2,0,1:T(8,128)(2,1)} %get-tuple-element.11), channel_id=1, source_target_pairs={{0,31},{1,0},{2,1},{3,2},{4,3},{5,4},{6,5},{7,6},{8,7},{9,8},{10,9... | collective-permute-start | bytes 1769480 | tf_op jit(solution)/shard_map/ppermute | solution.py:12

commit v2 on v1

v2 whole, which is shorter than its diff:
```python
import functools
import itertools

import jax
import jax.numpy as jnp
import numpy as np
from jax import lax
from jax.experimental import pallas as pl
from jax.experimental.pallas import tpu as pltpu
from jax.sharding import PartitionSpec as P

AXES = ("func", "box")
REACH = 3
SLOT = 32
STEP = 8


def passed_along(value, steps):
    count = lax.axis_size(AXES)
    pairs = [(source, (source + steps) % count) for source in range(count)]
    return lax.ppermute(value, AXES, pairs)


def rounded_up(value, multiple):
    return -(-int(value) // multiple) * multiple


@functools.lru_cache(maxsize=None)
def bounds(fun_dev, support):
    box_dev = fun_dev // 2
    orders = [
        order
        for order in sorted(set(itertools.permutations((1, 1, 2, 4))))
        if np.abs(np.cumsum(np.array(order) - 2)).max() <= 1
    ]
    box_all, fun_all = 12 * support, 24 * support
    assert fun_all % fun_dev == 0
    devices = fun_all // fun_dev
    rows = np.zeros(2 * REACH + 1, np.int64)
    low, high, boxes, end = 10**6, -(10**6), 0, 0
    for picks in itertools.product(orders, repeat=3):
        density = np.repeat(np.concatenate(picks), support)
        centers = np.repeat(np.arange(box_all), density)
        load = sum(np.roll(density, t) for t in range(support))
        below = np.concatenate([[0], np.cumsum(np.tile(load, 3))])
        over = np.clip(np.arange(box_all)[:, None] + support - box_all, 0, None)
        carried = int((over[:, 0] * density).sum())
        below = below - carried
        twice = below[:-1] + below[1:]
        cut = np.array([
            np.searchsorted(twice, 2 * support * fun_dev * (devices + d), side="right")
            for d in range(-REACH - 1, devices + REACH + 2)
        ]) - box_all
        first = REACH + 1
        width = np.diff(cut)
        place = cut - box_dev * (np.arange(len(cut)) - first)
        low, high = min(low, place.min()), max(high, place.max())
        boxes = max(boxes, width.max())
        end = max(end, (place[:-1] + width).max())
        box = centers[:, None] + np.arange(support)
        owner = np.searchsorted(cut, box, side="right") - 1 - first
        device = np.arange(fun_all)[:, None] // fun_dev
        offset = owner - device
        assert np.abs(offset).max() <= REACH
        count = np.bincount((device * (2 * REACH + 1) + offset + REACH).ravel(), minlength=devices * (2 * REACH + 1))
        rows = np.maximum(rows, count.reshape(devices, -1).max(0))
    return (
        tuple(rounded_up(r, 16) for r in rows),
        int(low),
        int(high),
        rounded_up(boxes, STEP),
        -(-int(end) // box_dev),
    )


def before(counts):
    return jnp.cumsum(counts, axis=-1) - counts


def unpack_kernel(slots, width_ref, column_ref, keep_ref, *refs):
    sources = refs[:slots]
    window_ref, gram_ref, total = refs[slots:]
    step = pl.program_id(0)
    first = step * STEP

    @pl.when(step == 0)
    def _():
        total[...] = jnp.zeros_like(total)

    @pl.when(first < width_ref[0])
    def _():
        for e in range(slots):
            start = column_ref[e * SLOT : (e + 1) * SLOT, 0:1]
            low = column_ref[e * SLOT : (e + 1) * SLOT, 1:2]
            high = column_ref[e * SLOT : (e + 1) * SLOT, 2:3]
            rows = sources[e].shape[0]
            lane = lax.broadcasted_iota(jnp.int32, (SLOT, rows), 1)
            picks = []
            for b in range(STEP):
                box = first + b
                row = jnp.where((box >= low) & (box < high), start + box, -1)
                picks.append((lane == row).astype(jnp.float32).astype(jnp.bfloat16))
            pick = jnp.concatenate(picks, axis=0)
            found = jnp.dot(pick, sources[e][...], preferred_element_type=jnp.float32)
            window_ref[:, e * SLOT : (e + 1) * SLOT, :] = found.astype(jnp.bfloat16).reshape(
                STEP, SLOT, found.shape[-1]
            )
        for b in range(STEP):
            here = window_ref[b]
            total[...] += lax.dot_general(
                here, here, (((1,), (1,)), ((), ())), preferred_element_type=jnp.float32
            )

    @pl.when(step == pl.num_programs(0) - 1)
    def _():
        keep = keep_ref[...]
        half = jnp.dot(total[...], keep, precision=lax.Precision.HIGHEST, preferred_element_type=jnp.float32)
        gram_ref[...] = lax.dot_general(
            keep, half, (((0,), (0,)), ((), ())), precision=lax.Precision.HIGHEST,
            preferred_element_type=jnp.float32,
        )


def mix_kernel(slots, width_ref, mixing_ref, place_ref, window_ref, *refs):
    outs = refs[:slots]
    mixed = refs[slots]
    step = pl.program_id(0)

    @pl.when(step == 0)
    def _():
        for out in outs:
            out[...] = jnp.zeros_like(out)

    @pl.when(step * STEP < width_ref[0])
    def _():
        for b in range(STEP):
            mixed[b] = jnp.dot(
                mixing_ref[...], window_ref[b], preferred_element_type=jnp.float32
            ).astype(jnp.bfloat16)
        for e in range(slots):
            rows = outs[e].shape[0]
            wanted = lax.broadcasted_iota(jnp.int32, (rows, STEP * SLOT), 0)
            pick = (wanted == place_ref[0, e : e + 1, :]).astype(jnp.float32).astype(jnp.bfloat16)
            part = mixed[:, e * SLOT : (e + 1) * SLOT, :].reshape(STEP * SLOT, mixed.shape[-1])
            outs[e][...] += jnp.dot(pick, part, preferred_element_type=jnp.float32).astype(jnp.bfloat16)


def home_kernel(slots, bases, column_ref, *refs):
    sources = refs[:slots]
    out_ref = refs[slots]
    row = column_ref[:, 0:1]
    value = None
    for e in range(slots):
        rows = sources[e].shape[0]
        lane = lax.broadcasted_iota(jnp.int32, (column_ref.shape[0], rows), 1)
        pick = (lane == row - bases[e]).astype(jnp.float32).astype(jnp.bfloat16)
        term = jnp.dot(pick, sources[e][...], preferred_element_type=jnp.float32)
        value = term if value is None else value + term
    out_ref[...] = value.astype(jnp.bfloat16)


def whole(shape):
    return pl.BlockSpec(shape, lambda g: (0,) * len(shape))


def on_device(coeffs, centers, kinetic, potential):
    fun_dev, support, points = coeffs.shape
    devices = lax.axis_size(AXES)
    me = lax.axis_index(AXES)
    fun_all = fun_dev * devices
    box_dev = fun_dev // 2
    box_all = box_dev * devices
    volume = 1.0 / (support * points)
    reading = 4 * support
    slots = 2 * REACH + 1
    offsets = list(range(-REACH, REACH + 1))
    order = sorted(offsets, key=lambda k: (abs(abs(k) - 1.9), k))
    window = slots * fun_dev
    rows, low_cut, high_cut, boxes, blocks = bounds(fun_dev, support)
    rows_of = {k: rows[k + REACH] for k in offsets}
    flat = coeffs.reshape(fun_dev * support, points)

    halo = REACH + -(-(reading + 8) // fun_dev)
    ahead = halo + 2
    around = jnp.concatenate(
        [centers[fun_all - halo * fun_dev :], centers, centers[: ahead * fun_dev]]
    )
    near = lax.dynamic_slice_in_dim(around, me * fun_dev, (halo + ahead) * fun_dev)
    near = (near - me * box_dev + box_all // 2) % box_all - box_all // 2
    sides = jnp.arange(-REACH, REACH + 2, dtype=jnp.int32)
    tries = low_cut + jnp.arange(high_cut - low_cut + 1, dtype=jnp.int32)
    tried = sides[:, None] * box_dev + tries[None, :]
    gap = tried[..., None] - near
    twice = jnp.sum(jnp.clip(gap, 0, support) + jnp.clip(gap + 1, 0, support), axis=-1)
    goal = 2 * support * fun_dev * (halo + sides)
    cut = low_cut + sides * box_dev + jnp.sum((twice <= goal[:, None]).astype(jnp.int32), axis=-1)

    mine = near[halo * fun_dev : (halo + 1) * fun_dev]
    edge = jnp.clip(cut[:, None] - mine[None, :], 0, support)
    leave = edge[1:] - edge[:-1]
    leave_at = before(leave)
    steps = jnp.arange(support, dtype=jnp.int32)
    goes = (steps >= edge[:-1, :, None]) & (steps < edge[1:, :, None])
    row_out = jnp.where(goes, leave_at[..., None] + steps - edge[:-1, :, None], -1)
    row_out = row_out.reshape(slots, fun_dev * support)

    arrived = {}
    for k in order:
        if k == 0:
            continue
        pick = (jnp.arange(rows_of[k], dtype=jnp.int32)[:, None] == row_out[k + REACH]).astype(jnp.bfloat16)
        packed = jnp.dot(pick, flat, preferred_element_type=jnp.float32).astype(jnp.bfloat16)
        arrived[k] = passed_along(packed, k)

    bases, total_rows = {}, 0
    for k in offsets:
        bases[k] = total_rows
        total_rows += rows_of[k]
    base_of = jnp.array([bases[k] for k in offsets], jnp.int32)
    home_row = jnp.sum(
        jnp.where(row_out >= 0, row_out + base_of[:, None], 0), axis=0
    )
    home_column = jnp.broadcast_to(home_row[:, None], (fun_dev * support, 8))

    others = near[(halo - REACH) * fun_dev : (halo + REACH + 1) * fun_dev].reshape(slots, fun_dev)
    start_cut, end_cut = cut[REACH], cut[REACH + 1]
    width = end_cut - start_cut
    edge_low = jnp.clip(start_cut - others, 0, support)
    edge_high = jnp.clip(end_cut - others, 0, support)
    come_at = before(edge_high - edge_low)
    box_low = edge_low + others - start_cut
    box_high = edge_high + others - start_cut
    packed_start = come_at - box_low
    own = jnp.arange(slots)[:, None] == REACH
    local_start = jnp.arange(fun_dev, dtype=jnp.int32)[None, :] * support + start_cut - others
    unpack_start = jnp.where(own, local_start, packed_start)
    columns = jnp.stack([unpack_start, box_low, box_high], axis=-1)
    columns = jnp.pad(columns, ((0, 0), (0, SLOT - fun_dev), (0, 5))).reshape(slots * SLOT, 8)
    box_range = jnp.arange(boxes, dtype=jnp.int32)[None, :, None]
    lies = (box_range >= box_low[:, None, :]) & (box_range < box_high[:, None, :])
    place = jnp.where(lies, packed_start[:, None, :] + box_range, -1)
    place = jnp.pad(place, ((0, 0), (0, 0), (0, SLOT - fun_dev)), constant_values=-1)
    place_rows = place.reshape(slots, boxes // STEP, STEP * SLOT).transpose(1, 0, 2)

    keep = np.zeros((slots * SLOT, window), np.float32)
    for e in range(slots):
        for f in range(fun_dev):
            keep[e * SLOT + f, e * fun_dev + f] = 1.0
    wide = slots * SLOT
    sources = [flat if e == REACH else arrived[REACH - e] for e in range(slots)]
    width_of = width.reshape(1)
    smem = pl.BlockSpec(memory_space=pltpu.SMEM)
    block = pl.BlockSpec((STEP, wide, points), lambda g: (g, 0, 0))
    pieces, partial = pl.pallas_call(
        functools.partial(unpack_kernel, slots),
        grid=(boxes // STEP,),
        out_shape=(
            jax.ShapeDtypeStruct((boxes, wide, points), jnp.bfloat16),
            jax.ShapeDtypeStruct((window, window), jnp.float32),
        ),
        in_specs=[smem, whole(columns.shape), whole(keep.shape)] + [whole(s.shape) for s in sources],
        out_specs=(block, whole((window, window))),
        scratch_shapes=[pltpu.VMEM((wide, wide), jnp.float32)],
        compiler_params=pltpu.CompilerParams(vmem_limit_bytes=48 * 2**20),
        name="unpack",
    )(width_of, columns, jnp.asarray(keep), *sources)
    partial = volume * partial

    waited, _ = lax.optimization_barrier((potential, tuple(arrived.values())))
    nearby = [waited if t == 0 else passed_along(waited, -t) for t in range(blocks)]
    nearby = jnp.pad(jnp.concatenate(nearby), ((0, max(0, high_cut + boxes - blocks * box_dev)), (0, 0)))
    region = lax.dynamic_slice_in_dim(nearby, start_cut, boxes)

    gram_rows = 0.0
    for k in order:
        at = (REACH - k) * fun_dev
        if k == 0:
            other = partial[at : at + fun_dev]
        else:
            sent_at = (REACH + k) * fun_dev
            other = passed_along(partial[sent_at : sent_at + fun_dev], k)
        gram_rows = gram_rows + jnp.pad(other, ((0, 0), (at, 2 * REACH * fun_dev - at)))
    first = 2 * REACH * fun_dev - (reading - 1)
    gram_band = jnp.stack([gram_rows[r, first + r : first + r + 2 * reading] for r in range(fun_dev)])
    gram_band = jnp.where(jnp.arange(2 * reading) < 2 * reading - 1, gram_band, 0.0)
    eye = jnp.eye(fun_dev, gram_rows.shape[1], 2 * REACH * fun_dev, dtype=jnp.float32)
    correction_rows = (1.5 * eye - 0.5 * gram_rows).astype(jnp.bfloat16)
    mixing_rows = [None] * slots
    for k in order:
        at = (REACH + k) * fun_dev
        sent = correction_rows[:, at : at + window]
        mixing_rows[REACH - k] = sent if k == 0 else passed_along(sent, k)
    correction = jnp.stack(mixing_rows)
    spaced = jnp.pad(
        correction.reshape(slots, fun_dev, slots, fun_dev),
        ((0, 0), (0, SLOT - fun_dev), (0, 0), (0, SLOT - fun_dev)),
    ).reshape(wide, wide)

    out_rows = [rows_of[REACH - e] for e in range(slots)]
    packed = pl.pallas_call(
        functools.partial(mix_kernel, slots),
        grid=(boxes // STEP,),
        out_shape=tuple(jax.ShapeDtypeStruct((r, points), jnp.bfloat16) for r in out_rows),
        in_specs=[
            smem,
            whole((wide, wide)),
            pl.BlockSpec((1, slots, STEP * SLOT), lambda g: (g, 0, 0)),
            block,
        ],
        out_specs=tuple(whole((r, points)) for r in out_rows),
        scratch_shapes=[pltpu.VMEM((STEP, wide, points), jnp.bfloat16)],
        compiler_params=pltpu.CompilerParams(vmem_limit_bytes=48 * 2**20),
        name="mix",
    )(width_of, spaced, place_rows, pieces)

    returned = {}
    for k in order:
        e = REACH - k
        here = packed[e]
        at_box = jnp.any(
            place[e][None] == jnp.arange(rows_of[k], dtype=jnp.int32)[:, None, None], axis=-1
        ).astype(jnp.float32)
        local = jnp.dot(at_box, region, precision=lax.Precision.HIGHEST)
        applied = jnp.dot(here, kinetic, preferred_element_type=jnp.float32)
        applied = (applied + local * here.astype(jnp.float32)).astype(jnp.bfloat16)
        returned[k] = applied if k == 0 else passed_along(applied, -k)

    parts = fun_dev * support // 256
    filtered = pl.pallas_call(
        functools.partial(home_kernel, slots, [bases[k] for k in offsets]),
        grid=(parts,),
        out_shape=jax.ShapeDtypeStruct((fun_dev * support, points), jnp.bfloat16),
        in_specs=[pl.BlockSpec((256, 8), lambda g: (g, 0))] + [whole((rows_of[k], points)) for k in offsets],
        out_specs=pl.BlockSpec((256, points), lambda g: (g, 0)),
        compiler_params=pltpu.CompilerParams(vmem_limit_bytes=32 * 2**20),
        name="home",
    )(home_column, *[returned[k] for k in offsets])
    return (filtered.reshape(coeffs.shape), gram_band)


def solution(mesh):
    placed = (P(AXES, None, None), P(), P(), P(AXES, None))
    return jax.shard_map(
        on_device,
        mesh=mesh,
        in_specs=placed,
        out_specs=(P(AXES, None, None), P(AXES, None)),
        check_vma=False,
    )
```

time: 171 us -> 163 us (0.953)
  the two profiles are of different devices: /device:TPU:1 before, /device:TPU:26 now
where the time goes in v2:
time: 163 us; the launch traced here: 162 us
  starting transfers between devices  48.3 us (30%)
  waiting for transfers between devices  31.1 us (19%)
  matrix products  23.9 us (15%)
  other arithmetic  19.6 us (12%)
  Pallas kernels  19.4 us (12%)
  local copies, waits for them, and re-layouts  15.4 us (9%)
  between operations  4.04 us (2%)
    ppermute x27, starting transfers between devices, passed_along(): return lax.ppermute(value, AXES, pairs)  48.3 us
    ppermute x27, waiting for transfers between devices, passed_along(): return lax.ppermute(value, AXES, pairs)  31.1 us
    dot_general x6, matrix products, on_device(): jnp.dot(pick, flat, preferred_element_type=jnp.float32).astype(jnp.bfloat16)  15.5 us
    pallas_call x1, Pallas kernels, on_device(): pl.pallas_call(functools.partial(unpack_kernel, slots), grid=(boxes // ST...  8.38 us
    reduce_or x5, other arithmetic, on_device(): jnp.any(place[e][None] == jnp.arange(rows_of[k], dtype=jnp.int32)[:, None...  7.76 us
    pallas_call x1, Pallas kernels, on_device(): pl.pallas_call(functools.partial(mix_kernel, slots), grid=(boxes // STEP,...  6.31 us
    pallas_call x1, Pallas kernels, on_device(): pl.pallas_call(functools.partial(home_kernel, slots, [bases[k] for k in o...  4.74 us
    dot_general x7, matrix products, on_device(): applied = jnp.dot(here, kinetic, preferred_element_type=jnp.float32)  4.66 us
  transfers between devices with their start and end apart: 27, of which 7 were waited for; matrix products, arithmetic and copies ran while one was open for 29% of the time, Pallas kernels for 4%

profile of v2, /device:TPU:26, one launch (start us, length us, event | category | flops | bytes accessed | tf_op | source)
XLA Modules:
  0.0 161.7 jit_solution(7566167564002663896)
XLA Ops:
  6.5 2.6 %convolution_convert_fusion.2 = bf16[160,1024]{1,0:T(8,128)(2,1)} fusion(bf16[768,1024]{1,0:T(8,128)(2,1)} %bitcast.61, s32[768]{0:T(1024)S(1)} %eq.227), kind=kOutput, calls=%fused_computation.15 | convolution fusion | flops 251944960 | bytes 1903616 | tf_op jit(solution)/shard_map/dot_general | solution.py:212
  9.7 2.6 %convolution_convert_fusion.3 = bf16[160,1024]{1,0:T(8,128)(2,1)} fusion(bf16[768,1024]{1,0:T(8,128)(2,1)} %bitcast.62, s32[768]{0:T(1024)S(1)} %eq.215), kind=kOutput, calls=%fused_computation.16 | convolution fusion | flops 251944960 | bytes 1903616 | tf_op jit(solution)/shard_map/dot_general | solution.py:212
  12.2 2.4 %collective-permute-start.1 = (bf16[160,1024]{1,0:T(8,128)(2,1)}, bf16[160,1024]{1,0:T(8,128)(2,1)}, u32[]{:S(2)}, u32[]{:S(2)}) collective-permute-start(bf16[160,1024]{1,0:T(8,128)(2,1)} %convolution_convert_fusion.3), channel_id=1, source_target_pairs={{0,2},{1,3},{2,4},{3,5},{4,6},{5,7},{6,8},{7,9},{8,10},{9,11},{10,... | collective-permute-start | bytes 983048 | tf_op jit(solution)/shard_map/ppermute | solution.py:21
  14.7 2.8 %convolution_convert_fusion = bf16[256,1024]{1,0:T(8,128)(2,1)} fusion(bf16[768,1024]{1,0:T(8,128)(2,1)} %bitcast.63, s32[768]{0:T(1024)S(1)} %eq.223), kind=kOutput, calls=%fused_computation.8 | convolution fusion | flops 403111936 | bytes 2100224 | tf_op jit(solution)/shard_map/dot_general | solution.py:212
  17.6 2.7 %convolution_convert_fusion.1 = bf16[240,1024]{1,0:T(8,128)(2,1)} fusion(bf16[768,1024]{1,0:T(8,128)(2,1)} %bitcast.64, s32[768]{0:T(1024)S(1)} %eq.219), kind=kOutput, calls=%fused_computation.10 | convolution fusion | flops 377917440 | bytes 2067456 | tf_op jit(solution)/shard_map/dot_general | solution.py:212
  20.9 2.4 %convolution_convert_fusion.4 = bf16[48,1024]{1,0:T(8,128)(2,1)} fusion(bf16[768,1024]{1,0:T(8,128)(2,1)} %bitcast.65, s32[768]{0:T(1024)S(1)} %eq.231), kind=kOutput, calls=%fused_computation.25 | convolution fusion | flops 75583488 | bytes 1674240 | tf_op jit(solution)/shard_map/dot_general | solution.py:212
  23.3 4.2 %collective-permute-start.5 = (bf16[48,1024]{1,0:T(8,128)(2,1)}, bf16[48,1024]{1,0:T(8,128)(2,1)S(1)}, u32[]{:S(2)}, u32[]{:S(2)}) collective-permute-start(bf16[48,1024]{1,0:T(8,128)(2,1)} %convolution_convert_fusion.4), channel_id=1, source_target_pairs={{0,29},{1,30},{2,31},{3,0},{4,1},{5,2},{6,3},{7,4},{8,5},{9,6},{10... | collective-permute-start | bytes 294920 | tf_op jit(solution)/shard_map/ppermute | solution.py:21
  35.1 1.9 %select_bitcast_fusion = (s32[7,24,1]{1,0,2:T(8,128)}, s32[7,24]{1,0:T(8,128)S(1)}, s32[7,24]{1,0:T(8,128)S(1)}) fusion(s32[7,24]{1,0:T(8,128)} %copy-done.5, s32[24]{0:T(128)} %multiply_add_fusion, pred[7]{0:T(512)(128)(4,1)} %iota_compare_fusion.25, s32[7,24]{1,0:T(8,128)} %reduce_window_sum.18, s32[7,24]{1,0:T(8,128)} %get-tuple-element.81, s32[]{:T(128)} %bitcast.1), kind=kLoop, calls=%fused_computation.100 | loop fusion | flops 1344 | bytes 4139 | tf_op jit(solution)/shard_map/stack | solution.py:237
  39.7 2.4 %convolution_convert_fusion.5 = bf16[48,1024]{1,0:T(8,128)(2,1)} fusion(bf16[768,1024]{1,0:T(8,128)(2,1)} %bitcast.66, s32[768]{0:T(1024)} %eq.211), kind=kOutput, calls=%fused_computation.26 | convolution fusion | flops 75583488 | bytes 1674240 | tf_op jit(solution)/shard_map/dot_general | solution.py:212
  42.1 1.8 %fusion.7 = (pred[160,24]{0,1:T(8,128)(4,1)}, pred[160,24]{0,1:T(8,128)(4,1)}) fusion(s32[24,32]{1,0:T(8,128)} %get-tuple-element.36, s32[24,32]{1,0:T(8,128)} %get-tuple-element.40), kind=kLoop, calls=%fused_computation.32 | loop fusion | flops 483840 | bytes 13824 | tf_op jit(solution)/shard_map/reduce_or | solution.py:320
  54.0 3.3 %collective-permute-done.refs_0_ = bf16[48,1024]{1,0:T(8,128)(2,1)S(1)} collective-permute-done((bf16[48,1024]{1,0:T(8,128)(2,1)}, bf16[48,1024]{1,0:T(8,128)(2,1)S(1)}, u32[]{:S(2)}, u32[]{:S(2)}) %collective-permute-start) | collective-permute-done | bytes 98336 | tf_op jit(solution)/shard_map/ppermute | solution.py:21
  59.7 8.4 %unpack.1 = (bf16[24,224,1024]{2,1,0:T(8,128)(2,1)}, f32[168,168]{1,0:T(8,128)S(1)}) custom-call(s32[1]{0:T(128)} %bitcast.2.width_ref, s32[224,8]{1,0:T(8,128)S(1)} %bitcast.68, f32[224,168]{1,0:T(8,128)S(1)} %copy-done.2, bf16[48,1024]{1,0:T(8,128)(2,1)S(1)} %collective-permute-done.refs_0_, bf16[160,1024]{1,0:T(8,128)(2,1)} %collective-permute-done.1.refs_1_, ...), custom_call_target="tpu_custom_call" | custom-call | tf_op jit(solution)/shard_map/unpack/pallas_call | solution.py:254
  68.1 2.9 %collective-permute-start.11 = (f32[24,168]{1,0:T(8,128)S(1)}, f32[24,168]{1,0:T(8,128)S(1)}, u32[]{:S(2)}, u32[]{:S(2)}) collective-permute-start(f32[24,168]{1,0:T(8,128)S(1)} %get-tuple-element.29), channel_id=1, source_target_pairs={{0,3},{1,4},{2,5},{3,6},{4,7},{5,8},{6,9},{7,10},{8,11},{9,12},{10... | collective-permute-start | bytes 48392 | tf_op jit(solution)/shard_map/ppermute | solution.py:21
  72.8 8.0 %collective-permute-start.7 = (f32[24,168]{1,0:T(8,128)S(1)}, f32[24,168]{1,0:T(8,128)S(1)}, u32[]{:S(2)}, u32[]{:S(2)}) collective-permute-start(f32[24,168]{1,0:T(8,128)S(1)} %get-tuple-element.33), channel_id=1, source_target_pairs={{0,2},{1,3},{2,4},{3,5},{4,6},{5,7},{6,8},{7,9},{8,10},{9,11},{10,... | collective-permute-start | bytes 48392 | tf_op jit(solution)/shard_map/ppermute | solution.py:21
  86.0 2.6 %collective-permute-start.12 = (bf16[24,168]{1,0:T(8,128)(2,1)S(1)}, bf16[24,168]{1,0:T(8,128)(2,1)S(1)}, u32[]{:S(2)}, u32[]{:S(2)}) collective-permute-start(bf16[24,168]{1,0:T(8,128)(2,1)S(1)} %get-tuple-element.77), channel_id=1, source_target_pairs={{0,3},{1,4},{2,5},{3,6},{4,7},{5,8},{6,9},{7,10},{8,11},{9,12},{10... | collective-permute-start | bytes 24200 | tf_op jit(solution)/shard_map/ppermute | solution.py:21
  88.5 5.9 %collective-permute-start.13 = (bf16[24,168]{1,0:T(8,128)(2,1)S(1)}, bf16[24,168]{1,0:T(8,128)(2,1)S(1)}, u32[]{:S(2)}, u32[]{:S(2)}) collective-permute-start(bf16[24,168]{1,0:T(8,128)(2,1)S(1)} %get-tuple-element.76), channel_id=1, source_target_pairs={{0,2},{1,3},{2,4},{3,5},{4,6},{5,7},{6,8},{7,9},{8,10},{9,11},{10,... | collective-permute-start | bytes 24200 | tf_op jit(solution)/shard_map/ppermute | solution.py:21
  95.2 4.0 %collective-permute-start.14 = (bf16[24,168]{1,0:T(8,128)(2,1)S(1)}, bf16[24,168]{1,0:T(8,128)(2,1)S(1)}, u32[]{:S(2)}, u32[]{:S(2)}) collective-permute-start(bf16[24,168]{1,0:T(8,128)(2,1)S(1)} %get-tuple-element.75), channel_id=1, source_target_pairs={{0,1},{1,2},{2,3},{3,4},{4,5},{5,6},{6,7},{7,8},{8,9},{9,10},{10,1... | collective-permute-start | bytes 24200 | tf_op jit(solution)/shard_map/ppermute | solution.py:21
  103.0 3.6 %collective-permute-done.16 = bf16[24,168]{1,0:T(8,128)(2,1)S(1)} collective-permute-done((bf16[24,168]{1,0:T(8,128)(2,1)S(1)}, bf16[24,168]{1,0:T(8,128)(2,1)S(1)}, u32[]{:S(2)}, u32[]{:S(2)}) %collective-permute-start.16) | collective-permute-done | bytes 8096 | tf_op jit(solution)/shard_map/ppermute | solution.py:21
  106.8 2.2 %collective-permute-done.17 = bf16[24,168]{1,0:T(8,128)(2,1)S(1)} collective-permute-done((bf16[24,168]{1,0:T(8,128)(2,1)S(1)}, bf16[24,168]{1,0:T(8,128)(2,1)S(1)}, u32[]{:S(2)}, u32[]{:S(2)}) %collective-permute-start.17) | collective-permute-done | bytes 8096 | tf_op jit(solution)/shard_map/ppermute | solution.py:21
  109.5 6.3 %mix.1 = (bf16[48,1024]{1,0:T(8,128)(2,1)S(1)}, bf16[160,1024]{1,0:T(8,128)(2,1)S(1)}, bf16[240,1024]{1,0:T(8,128)(2,1)S(1)}, bf16[512,1024]{1,0:T(8,128)(2,1)S(...) custom-call(s32[1]{0:T(128)} %bitcast.2.width_ref, ...), custom_call_target="tpu_custom_call" | custom-call | tf_op jit(solution)/shard_map/mix/pallas_call | solution.py:300
  116.8 4.6 %collective-permute-start.21 = (bf16[48,1024]{1,0:T(8,128)(2,1)S(1)}, bf16[48,1024]{1,0:T(8,128)(2,1)S(1)}, u32[]{:S(2)}, u32[]{:S(2)}) collective-permute-start(bf16[48,1024]{1,0:T(8,128)(2,1)S(1)} %fusion.5), channel_id=1, source_target_pairs={{0,3},{1,4},{2,5},{3,6},{4,7},{5,8},{6,9},{7,10},{8,11},{9,12},{10... | collective-permute-start | bytes 294920 | tf_op jit(solution)/shard_map/ppermute | solution.py:21
  122.4 6.9 %collective-permute-start.22 = (bf16[160,1024]{1,0:T(8,128)(2,1)S(1)}, bf16[160,1024]{1,0:T(8,128)(2,1)S(1)}, u32[]{:S(2)}, u32[]{:S(2)}) collective-permute-start(bf16[160,1024]{1,0:T(8,128)(2,1)S(1)} %fusion.3), channel_id=1, source_target_pairs={{0,2},{1,3},{2,4},{3,5},{4,6},{5,7},{6,8},{7,9},{8,10},{9,11},{10,... | collective-permute-start | bytes 983048 | tf_op jit(solution)/shard_map/ppermute | solution.py:21
  138.1 18.8 %collective-permute-done.26.refs_6_ = bf16[48,1024]{1,0:T(8,128)(2,1)S(1)} collective-permute-done((bf16[48,1024]{1,0:T(8,128)(2,1)S(1)}, bf16[48,1024]{1,0:T(8,128)(2,1)S(1)}, u32[]{:S(2)}, u32[]{:S(2)}) %collective-permute-start.26) | collective-permute-done | bytes 98336 | tf_op jit(solution)/shard_map/ppermute | solution.py:21
  157.0 4.7 %home.1 = bf16[768,1024]{1,0:T(8,128)(2,1)} custom-call(s32[768,8]{1,0:T(8,128)S(1)} %broadcast_in_dim.26.column_ref, bf16[48,1024]{1,0:T(8,128)(2,1)S(1)} %collective-permute-done.21.refs_0_, bf16[160,1024]{1,0:T(8,128)(2,1)S(1)} %collective-permute-done.22.refs_1_, bf16[256,1024]{1,0:T(8,128)(2,1)S(1)} %collective-permute-done.23.refs_2_, ...), custom_call_target="tpu_custom_call" | custom-call | tf_op jit(solution)/shard_map/home/pallas_call | solution.py:329
  (151 shorter events, 49.6 us)
Async XLA Ops:
  9.1 48.2 %collective-permute-start.4 = (bf16[160,1024]{1,0:T(8,128)(2,1)}, bf16[160,1024]{1,0:T(8,128)(2,1)S(1)}, u32[]{:S(2)}, u32[]{:S(2)}) collective-permute-start(bf16[160,1024]{1,0:T(8,128)(2,1)} %convolution_convert_fusion.2), channel_id=1, source_target_pairs={{0,30},{1,31},{2,0},{3,1},{4,2},{5,3},{6,4},{7,5},{8,6},{9,7},{10,... | collective-permute-start | bytes 983048 | tf_op jit(solution)/shard_map/ppermute | solution.py:21
  12.2 45.1 %collective-permute-start.1 = (bf16[160,1024]{1,0:T(8,128)(2,1)}, bf16[160,1024]{1,0:T(8,128)(2,1)}, u32[]{:S(2)}, u32[]{:S(2)}) collective-permute-start(bf16[160,1024]{1,0:T(8,128)(2,1)} %convolution_convert_fusion.3), channel_id=1, source_target_pairs={{0,2},{1,3},{2,4},{3,5},{4,6},{5,7},{6,8},{7,9},{8,10},{9,11},{10,... | collective-permute-start | bytes 983048 | tf_op jit(solution)/shard_map/ppermute | solution.py:21
  17.5 39.8 %collective-permute-start.3 = (bf16[256,1024]{1,0:T(8,128)(2,1)}, bf16[256,1024]{1,0:T(8,128)(2,1)S(1)}, u32[]{:S(2)}, u32[]{:S(2)}) collective-permute-start(bf16[256,1024]{1,0:T(8,128)(2,1)} %convolution_convert_fusion), channel_id=1, source_target_pairs={{0,31},{1,0},{2,1},{3,2},{4,3},{5,4},{6,5},{7,6},{8,7},{9,8},{10,9... | collective-permute-start | bytes 1572872 | tf_op jit(solution)/shard_map/ppermute | solution.py:21
  20.3 37.0 %collective-permute-start.2 = (bf16[240,1024]{1,0:T(8,128)(2,1)}, bf16[240,1024]{1,0:T(8,128)(2,1)S(1)}, u32[]{:S(2)}, u32[]{:S(2)}) collective-permute-start(bf16[240,1024]{1,0:T(8,128)(2,1)} %convolution_convert_fusion.1), channel_id=1, source_target_pairs={{0,1},{1,2},{2,3},{3,4},{4,5},{5,6},{6,7},{7,8},{8,9},{9,10},{10,1... | collective-permute-start | bytes 1474568 | tf_op jit(solution)/shard_map/ppermute | solution.py:21
  23.3 28.5 %collective-permute-start.5 = (bf16[48,1024]{1,0:T(8,128)(2,1)}, bf16[48,1024]{1,0:T(8,128)(2,1)S(1)}, u32[]{:S(2)}, u32[]{:S(2)}) collective-permute-start(bf16[48,1024]{1,0:T(8,128)(2,1)} %convolution_convert_fusion.4), channel_id=1, source_target_pairs={{0,29},{1,30},{2,31},{3,0},{4,1},{5,2},{6,3},{7,4},{8,5},{9,6},{10... | collective-permute-start | bytes 294920 | tf_op jit(solution)/shard_map/ppermute | solution.py:21
  51.8 5.5 %collective-permute-start = (bf16[48,1024]{1,0:T(8,128)(2,1)}, bf16[48,1024]{1,0:T(8,128)(2,1)S(1)}, u32[]{:S(2)}, u32[]{:S(2)}) collective-permute-start(bf16[48,1024]{1,0:T(8,128)(2,1)} %convolution_convert_fusion.5), channel_id=1, source_target_pairs={{0,3},{1,4},{2,5},{3,6},{4,7},{5,8},{6,9},{7,10},{8,11},{9,12},{10... | collective-permute-start | bytes 294920 | tf_op jit(solution)/shard_map/ppermute | solution.py:21
  68.1 12.7 %collective-permute-start.11 = (f32[24,168]{1,0:T(8,128)S(1)}, f32[24,168]{1,0:T(8,128)S(1)}, u32[]{:S(2)}, u32[]{:S(2)}) collective-permute-start(f32[24,168]{1,0:T(8,128)S(1)} %get-tuple-element.29), channel_id=1, source_target_pairs={{0,3},{1,4},{2,5},{3,6},{4,7},{5,8},{6,9},{7,10},{8,11},{9,12},{10... | collective-permute-start | bytes 48392 | tf_op jit(solution)/shard_map/ppermute | solution.py:21
  71.0 13.3 %collective-permute-start.10 = (f32[24,168]{1,0:T(8,128)S(1)}, f32[24,168]{1,0:T(8,128)S(1)}, u32[]{:S(2)}, u32[]{:S(2)}) collective-permute-start(f32[24,168]{1,0:T(8,128)S(1)} %get-tuple-element.30), channel_id=1, source_target_pairs={{0,29},{1,30},{2,31},{3,0},{4,1},{5,2},{6,3},{7,4},{8,5},{9,6},{10... | collective-permute-start | bytes 48392 | tf_op jit(solution)/shard_map/ppermute | solution.py:21
  71.0 13.4 %collective-permute-start.9 = (f32[24,168]{1,0:T(8,128)S(1)}, f32[24,168]{1,0:T(8,128)S(1)}, u32[]{:S(2)}, u32[]{:S(2)}) collective-permute-start(f32[24,168]{1,0:T(8,128)S(1)} %get-tuple-element.31), channel_id=1, source_target_pairs={{0,1},{1,2},{2,3},{3,4},{4,5},{5,6},{6,7},{7,8},{8,9},{9,10},{10,1... | collective-permute-start | bytes 48392 | tf_op jit(solution)/shard_map/ppermute | solution.py:21
  71.9 12.6 %collective-permute-start.8 = (f32[24,168]{1,0:T(8,128)S(1)}, f32[24,168]{1,0:T(8,128)S(1)}, u32[]{:S(2)}, u32[]{:S(2)}) collective-permute-start(f32[24,168]{1,0:T(8,128)S(1)} %get-tuple-element.32), channel_id=1, source_target_pairs={{0,31},{1,0},{2,1},{3,2},{4,3},{5,4},{6,5},{7,6},{8,7},{9,8},{10,9... | collective-permute-start | bytes 48392 | tf_op jit(solution)/shard_map/ppermute | solution.py:21
  72.8 11.8 %collective-permute-start.7 = (f32[24,168]{1,0:T(8,128)S(1)}, f32[24,168]{1,0:T(8,128)S(1)}, u32[]{:S(2)}, u32[]{:S(2)}) collective-permute-start(f32[24,168]{1,0:T(8,128)S(1)} %get-tuple-element.33), channel_id=1, source_target_pairs={{0,2},{1,3},{2,4},{3,5},{4,6},{5,7},{6,8},{7,9},{8,10},{9,11},{10,... | collective-permute-start | bytes 48392 | tf_op jit(solution)/shard_map/ppermute | solution.py:21
  84.3 31.5 %collective-permute-start.18 = (f32[12,1024]{1,0:T(8,128)}, f32[12,1024]{1,0:T(8,128)S(1)}, u32[]{:S(2)}, u32[]{:S(2)}) collective-permute-start(f32[12,1024]{1,0:T(8,128)} %param.9), channel_id=1, source_target_pairs={{0,31},{1,0},{2,1},{3,2},{4,3},{5,4},{6,5},{7,6},{8,7},{9,8},{10,9... | collective-permute-start | bytes 147464 | tf_op jit(solution)/shard_map/ppermute | solution.py:21
  84.4 31.4 %collective-permute-start.19 = (f32[12,1024]{1,0:T(8,128)}, f32[12,1024]{1,0:T(8,128)S(1)}, u32[]{:S(2)}, u32[]{:S(2)}) collective-permute-start(f32[12,1024]{1,0:T(8,128)} %param.9), channel_id=1, source_target_pairs={{0,30},{1,31},{2,0},{3,1},{4,2},{5,3},{6,4},{7,5},{8,6},{9,7},{10,... | collective-permute-start | bytes 147464 | tf_op jit(solution)/shard_map/ppermute | solution.py:21
  84.5 31.4 %collective-permute-start.20 = (f32[12,1024]{1,0:T(8,128)}, f32[12,1024]{1,0:T(8,128)S(1)}, u32[]{:S(2)}, u32[]{:S(2)}) collective-permute-start(f32[12,1024]{1,0:T(8,128)} %param.9), channel_id=1, source_target_pairs={{0,29},{1,30},{2,31},{3,0},{4,1},{5,2},{6,3},{7,4},{8,5},{9,6},{10... | collective-permute-start | bytes 147464 | tf_op jit(solution)/shard_map/ppermute | solution.py:21
  86.0 9.3 %collective-permute-start.12 = (bf16[24,168]{1,0:T(8,128)(2,1)S(1)}, bf16[24,168]{1,0:T(8,128)(2,1)S(1)}, u32[]{:S(2)}, u32[]{:S(2)}) collective-permute-start(bf16[24,168]{1,0:T(8,128)(2,1)S(1)} %get-tuple-element.77), channel_id=1, source_target_pairs={{0,3},{1,4},{2,5},{3,6},{4,7},{5,8},{6,9},{7,10},{8,11},{9,12},{10... | collective-permute-start | bytes 24200 | tf_op jit(solution)/shard_map/ppermute | solution.py:21
  88.5 10.9 %collective-permute-start.13 = (bf16[24,168]{1,0:T(8,128)(2,1)S(1)}, bf16[24,168]{1,0:T(8,128)(2,1)S(1)}, u32[]{:S(2)}, u32[]{:S(2)}) collective-permute-start(bf16[24,168]{1,0:T(8,128)(2,1)S(1)} %get-tuple-element.76), channel_id=1, source_target_pairs={{0,2},{1,3},{2,4},{3,5},{4,6},{5,7},{6,8},{7,9},{8,10},{9,11},{10,... | collective-permute-start | bytes 24200 | tf_op jit(solution)/shard_map/ppermute | solution.py:21
  100.4 6.2 %collective-permute-start.16 = (bf16[24,168]{1,0:T(8,128)(2,1)S(1)}, bf16[24,168]{1,0:T(8,128)(2,1)S(1)}, u32[]{:S(2)}, u32[]{:S(2)}) collective-permute-start(bf16[24,168]{1,0:T(8,128)(2,1)S(1)} %get-tuple-element.72), channel_id=1, source_target_pairs={{0,30},{1,31},{2,0},{3,1},{4,2},{5,3},{6,4},{7,5},{8,6},{9,7},{10,... | collective-permute-start | bytes 24200 | tf_op jit(solution)/shard_map/ppermute | solution.py:21
  101.9 7.1 %collective-permute-start.17 = (bf16[24,168]{1,0:T(8,128)(2,1)S(1)}, bf16[24,168]{1,0:T(8,128)(2,1)S(1)}, u32[]{:S(2)}, u32[]{:S(2)}) collective-permute-start(bf16[24,168]{1,0:T(8,128)(2,1)S(1)} %get-tuple-element.71), channel_id=1, source_target_pairs={{0,29},{1,30},{2,31},{3,0},{4,1},{5,2},{6,3},{7,4},{8,5},{9,6},{10... | collective-permute-start | bytes 24200 | tf_op jit(solution)/shard_map/ppermute | solution.py:21
  116.8 19.9 %collective-permute-start.21 = (bf16[48,1024]{1,0:T(8,128)(2,1)S(1)}, bf16[48,1024]{1,0:T(8,128)(2,1)S(1)}, u32[]{:S(2)}, u32[]{:S(2)}) collective-permute-start(bf16[48,1024]{1,0:T(8,128)(2,1)S(1)} %fusion.5), channel_id=1, source_target_pairs={{0,3},{1,4},{2,5},{3,6},{4,7},{5,8},{6,9},{7,10},{8,11},{9,12},{10... | collective-permute-start | bytes 294920 | tf_op jit(solution)/shard_map/ppermute | solution.py:21
  122.4 34.4 %collective-permute-start.22 = (bf16[160,1024]{1,0:T(8,128)(2,1)S(1)}, bf16[160,1024]{1,0:T(8,128)(2,1)S(1)}, u32[]{:S(2)}, u32[]{:S(2)}) collective-permute-start(bf16[160,1024]{1,0:T(8,128)(2,1)S(1)} %fusion.3), channel_id=1, source_target_pairs={{0,2},{1,3},{2,4},{3,5},{4,6},{5,7},{6,8},{7,9},{8,10},{9,11},{10,... | collective-permute-start | bytes 983048 | tf_op jit(solution)/shard_map/ppermute | solution.py:21
  130.7 26.2 %collective-permute-start.23 = (bf16[256,1024]{1,0:T(8,128)(2,1)S(1)}, bf16[256,1024]{1,0:T(8,128)(2,1)S(1)}, u32[]{:S(2)}, u32[]{:S(2)}) collective-permute-start(bf16[256,1024]{1,0:T(8,128)(2,1)S(1)} %fusion.1), channel_id=1, source_target_pairs={{0,1},{1,2},{2,3},{3,4},{4,5},{5,6},{6,7},{7,8},{8,9},{9,10},{10,1... | collective-permute-start | bytes 1572872 | tf_op jit(solution)/shard_map/ppermute | solution.py:21
  132.1 24.8 %collective-permute-start.24 = (bf16[240,1024]{1,0:T(8,128)(2,1)S(1)}, bf16[240,1024]{1,0:T(8,128)(2,1)S(1)}, u32[]{:S(2)}, u32[]{:S(2)}) collective-permute-start(bf16[240,1024]{1,0:T(8,128)(2,1)S(1)} %fusion.2), channel_id=1, source_target_pairs={{0,31},{1,0},{2,1},{3,2},{4,3},{5,4},{6,5},{7,6},{8,7},{9,8},{10,9... | collective-permute-start | bytes 1474568 | tf_op jit(solution)/shard_map/ppermute | solution.py:21
  134.8 22.0 %collective-permute-start.25 = (bf16[160,1024]{1,0:T(8,128)(2,1)S(1)}, bf16[160,1024]{1,0:T(8,128)(2,1)S(1)}, u32[]{:S(2)}, u32[]{:S(2)}) collective-permute-start(bf16[160,1024]{1,0:T(8,128)(2,1)S(1)} %fusion.4), channel_id=1, source_target_pairs={{0,30},{1,31},{2,0},{3,1},{4,2},{5,3},{6,4},{7,5},{8,6},{9,7},{10,... | collective-permute-start | bytes 983048 | tf_op jit(solution)/shard_map/ppermute | solution.py:21
  136.7 20.1 %collective-permute-start.26 = (bf16[48,1024]{1,0:T(8,128)(2,1)S(1)}, bf16[48,1024]{1,0:T(8,128)(2,1)S(1)}, u32[]{:S(2)}, u32[]{:S(2)}) collective-permute-start(bf16[48,1024]{1,0:T(8,128)(2,1)S(1)} %fusion.6), channel_id=1, source_target_pairs={{0,29},{1,30},{2,31},{3,0},{4,1},{5,2},{6,3},{7,4},{8,5},{9,6},{10... | collective-permute-start | bytes 294920 | tf_op jit(solution)/shard_map/ppermute | solution.py:21
  (15 other events, 164.1 us)
